TPU v7x, 512 devices: a whole 4x4x16 slice. The times are simulated.
512 devices in a mesh: dp: 16 (over z), expert: 32 (over x, y, core).
Axes of the slice: x: 4, y: 4, z: 16, core: 2. Of those that a mesh axis runs over, the one named last changes fastest.
Arguments:
- tokens: bfloat16 [65536, 1024], P(('dp', 'expert')), may hold values from -6 to 6
- route_ids: int32 [65536, 4], P(('dp', 'expert')), may hold values from 0 to 31, all different within a row; in each aligned block of 128 rows (0 to 127, 128 to 255, ...) at most 24 rows name the same one
- route_weights: float32 [65536, 4], P(('dp', 'expert')), may hold values from 0.2 to 1
- up_weight: bfloat16 [32, 1024, 704], P('expert', 'dp'), may hold values from -0.1875 to 0.1875
- down_weight: bfloat16 [32, 1024, 704], P('expert', 'dp'), may hold values from -0.21875 to 0.21875
- head_weight: bfloat16 [1024, 1024], P('dp'), may hold values from -0.75 to 0.75
- out_weight: float32 [1024], P('dp'), may hold values from -0.375 to 0.375
- pool_ids: int32 [512, 128], P(('dp', 'expert')), may hold values from 0 to 15, never falling along the last dimension, each value on 1 to 64 neighbouring positions
- list_ids: int32 [512, 16], P(('dp', 'expert')), may hold values from 0 to 7, as said below
- clicks: int32 [512, 16], P(('dp', 'expert')), may hold values 0 or 1
- ranks: int32 [512, 16], P(('dp', 'expert')), may hold values from 0 to 31
- alpha_table: float32 [32], replicated, may hold values from 0.3 to 1
- beta_table: float32 [32], replicated, may hold values from 0 to 0.3
Outputs:
- grad_up: bfloat16 [32, 1024, 704], P('expert', 'dp')
- grad_down: bfloat16 [32, 1024, 704], P('expert', 'dp')
- grad_head: float32 [1024, 1024], P('dp')
- grad_out: float32 [1024], P('dp')
- list_loss: float32 [32], P('expert')
Inputs may be any that keep to these rules, and one draw needn't show every extreme that they name: `route_ids`: each token names 4 different experts; among the 128 tokens of one device no expert is named more than 24 times, a bound that some block reaches. `pool_ids`: in each row the candidate number never falls, every candidate has 1 to 64 tokens and one has exactly 64. `list_ids`: every list number appears in every row.
All inputs are finite; a program needn't handle non-finite values. No bound on the sum of `clicks` on one device may be relied on, other than what follows from the above.
Results may differ from a plain program's by a relative error of at most 0.028.
Values may be sent and summed in bfloat16 or wider, within the bound.
A program may use at most 64 MiB of HBM per device.

v0:
```python
import jax
import jax.numpy as jnp
from jax import lax
from jax.sharding import PartitionSpec as P

LISTS = 8
RANKS = 32


def silu_slope(pre_act):
    sigmoid = jax.nn.sigmoid(pre_act)
    return sigmoid * (1.0 + pre_act * (1.0 - sigmoid))


def local(
    tokens,
    route_ids,
    route_weights,
    up_weight,
    down_weight,
    head_weight,
    out_weight,
    pool_ids,
    list_ids,
    clicks,
    ranks,
    alpha_table,
    beta_table,
):
    tok_count = tokens.shape[0]
    model_width = tokens.shape[1]
    top_count = route_ids.shape[1]
    owners = lax.axis_size("expert")
    capacity = 3 * tok_count * top_count // (2 * owners)
    slot_total = owners * capacity
    flat_ids = route_ids.reshape(-1)
    expert_hot = (flat_ids[:, None] == jnp.arange(owners, dtype=jnp.int32)[None, :]).astype(
        jnp.int32
    )
    running = jnp.cumsum(expert_hot, axis=0) - 1
    slot_index = jnp.sum(running * expert_hot, axis=1)
    target = flat_ids * capacity + slot_index
    token_index = jnp.arange(tok_count * top_count, dtype=jnp.int32) // top_count
    outgoing = (
        jnp.zeros((slot_total, model_width), jnp.bfloat16).at[target].set(tokens[token_index])
    )
    received = lax.all_to_all(
        outgoing.reshape(owners, capacity, model_width),
        "expert",
        split_axis=0,
        concat_axis=0,
        tiled=True,
    )
    inputs = received.reshape(slot_total, model_width)
    up_local = up_weight[0]
    down_local = down_weight[0]
    hidden_width = up_local.shape[1]
    columns = inputs
    pre_act = jnp.dot(
        columns,
        lax.all_gather(up_local, "dp", axis=0, tiled=True),
        preferred_element_type=jnp.float32,
    )
    activated = jax.nn.silu(pre_act).astype(jnp.bfloat16)
    expert_out = lax.dot_general(
        activated,
        lax.all_gather(down_local, "dp", axis=0, tiled=True),
        (((1,), (1,)), ((), ())),
        preferred_element_type=jnp.float32,
    ).astype(jnp.bfloat16)
    returned = lax.all_to_all(
        expert_out.reshape(owners, capacity, model_width),
        "expert",
        split_axis=0,
        concat_axis=0,
        tiled=True,
    ).reshape(slot_total, model_width)
    routed_rows = returned[target].reshape(tok_count, top_count, model_width)
    routed = jnp.sum(route_weights[:, :, None] * routed_rows.astype(jnp.float32), axis=1)
    mixed = tokens.astype(jnp.float32) + routed
    inv_rms = lax.rsqrt(jnp.mean(mixed * mixed, axis=1, keepdims=True) + 1e-06)
    normed = mixed * inv_rms
    cand_count = list_ids.shape[1]
    member = (pool_ids[0][:, None] == jnp.arange(cand_count, dtype=jnp.int32)[None, :]).astype(
        jnp.float32
    )
    token_counts = jnp.sum(member, axis=0)
    pooled_sum = lax.dot_general(
        member,
        normed,
        (((0,), (0,)), ((), ())),
        precision=lax.Precision.HIGHEST,
        preferred_element_type=jnp.float32,
    )
    pooled = (pooled_sum / token_counts[:, None]).astype(jnp.bfloat16)
    all_pooled = lax.all_gather(pooled, "dp", axis=0, tiled=True)
    head_act = jnp.tanh(
        lax.dot_general(
            all_pooled, head_weight, (((1,), (1,)), ((), ())), preferred_element_type=jnp.float32
        )
    )
    part_score = jnp.sum(head_act * out_weight[None, :], axis=1)
    rank_hot = (ranks[0][:, None] == jnp.arange(RANKS, dtype=jnp.int32)[None, :]).astype(
        jnp.float32
    )
    alpha_of = jnp.sum(rank_hot * alpha_table[None, :], axis=1)
    beta_of = jnp.sum(rank_hot * beta_table[None, :], axis=1)
    corrected = (clicks[0].astype(jnp.float32) - beta_of) / alpha_of
    list_hot = (list_ids[0][:, None] == jnp.arange(LISTS, dtype=jnp.int32)[None, :]).astype(
        jnp.float32
    )
    scores = lax.psum_scatter(part_score, "dp", scatter_dimension=0, tiled=True)
    exp_scores = jnp.exp(scores)
    exp_total, click_total, cross_total = lax.psum(
        (
            jnp.sum(exp_scores[:, None] * list_hot, axis=0),
            jnp.sum(corrected[:, None] * list_hot, axis=0),
            jnp.sum((corrected * scores)[:, None] * list_hot, axis=0),
        ),
        "dp",
    )
    list_loss = jnp.sum(click_total * jnp.log(exp_total) - cross_total).reshape(1)
    cand_grad = (
        jnp.sum(list_hot * (click_total / exp_total)[None, :], axis=1) * exp_scores - corrected
    )
    group_grad = lax.all_gather(cand_grad, "dp", axis=0, tiled=True)
    hid_grad = (group_grad[:, None] * out_weight[None, :] * (1.0 - head_act * head_act)).astype(
        jnp.bfloat16
    )
    head_term = lax.dot_general(
        hid_grad, all_pooled, (((0,), (0,)), ((), ())), preferred_element_type=jnp.float32
    )
    out_term = jnp.sum(group_grad[:, None] * head_act, axis=0)
    grad_head, grad_out = (
        lax.psum(head_term.astype(jnp.bfloat16), "expert").astype(jnp.float32),
        lax.psum(out_term.astype(jnp.bfloat16), "expert").astype(jnp.float32),
    )
    pooled_grad = lax.psum_scatter(
        jnp.dot(hid_grad, head_weight, preferred_element_type=jnp.float32).astype(jnp.bfloat16),
        "dp",
        scatter_dimension=0,
        tiled=True,
    ).astype(jnp.float32)
    normed_grad = jnp.dot(
        member,
        pooled_grad / token_counts[:, None],
        precision=lax.Precision.HIGHEST,
        preferred_element_type=jnp.float32,
    )
    mixed_grad = inv_rms * (
        normed_grad - normed * jnp.mean(normed_grad * normed, axis=1, keepdims=True)
    )
    cotangent = (
        (route_weights[:, :, None] * mixed_grad[:, None, :])
        .astype(jnp.bfloat16)
        .reshape(tok_count * top_count, model_width)
    )
    outgoing_grad = jnp.zeros((slot_total, model_width), jnp.bfloat16).at[target].set(cotangent)
    slot_grad = lax.all_to_all(
        outgoing_grad.reshape(owners, capacity, model_width),
        "expert",
        split_axis=0,
        concat_axis=0,
        tiled=True,
    ).reshape(slot_total, model_width)
    columns = slot_grad
    act_grad = jnp.dot(
        columns,
        lax.all_gather(down_local, "dp", axis=0, tiled=True),
        preferred_element_type=jnp.float32,
    )
    pre_grad = (act_grad * silu_slope(pre_act)).astype(jnp.bfloat16)
    up_term = lax.dot_general(
        inputs, pre_grad, (((0,), (0,)), ((), ())), preferred_element_type=jnp.float32
    )
    down_term = lax.dot_general(
        slot_grad, activated, (((0,), (0,)), ((), ())), preferred_element_type=jnp.float32
    )
    summed = lax.psum_scatter(
        jnp.concatenate([up_term, down_term], axis=1).astype(jnp.bfloat16),
        "dp",
        scatter_dimension=0,
        tiled=True,
    ).astype(jnp.float32)
    grad_up = summed[:, :hidden_width].astype(jnp.bfloat16)[None]
    grad_down = summed[:, hidden_width:].astype(jnp.bfloat16)[None]
    return (grad_up, grad_down, grad_head, grad_out, list_loss)


def solution(mesh):
    return jax.shard_map(
        local,
        mesh=mesh,
        in_specs=(
            P(("dp", "expert"), None),
            P(("dp", "expert"), None),
            P(("dp", "expert"), None),
            P("expert", "dp", None),
            P("expert", "dp", None),
            P("dp", None),
            P("dp"),
            P(("dp", "expert"), None),
            P(("dp", "expert"), None),
            P(("dp", "expert"), None),
            P(("dp", "expert"), None),
            P(),
            P(),
        ),
        out_specs=(
            P("expert", "dp", None),
            P("expert", "dp", None),
            P("dp", None),
            P("dp"),
            P("expert"),
        ),
        check_vma=False,
    )
```

profile of v0, /device:TPU:2, one launch (start us, length us, event | category | flops | bytes accessed | tf_op | source)
XLA Modules:
  0.0 616.2 jit_solution(5484869024064051022)
XLA Ops:
  7.2 0.7 all-gather.5.cloned.1.call-update
  8.0 0.7 all-gather.7.cloned.1.call-update
  8.7 0.7 broadcast_multiply_fusion
  9.4 0.8 copy.38
  10.1 0.1 eq.74
  10.2 0.1 eq.70
  10.4 0.1 copy.37
  10.5 0.1 mul.176
  10.6 1.2 reduce-window.6
  11.8 0.2 slice_reduce_fusion
  12.2 7.4 %scatter_custom_fusion = bf16[768,1024]{1,0:T(8,128)(2,1)S(1)} fusion(s32[512]{0:T(512)S(1)} %bitcast.67, bf16[128,1024]{1,0:T(8,128)(2,1)} %param.13, s32[1024]{0:T(1024)S(1)} %pad_clamp_fusion.1, bf16[]{:T(256)} %constant.40.clone.1), kind=kCustom, calls=%fused_computation.24 | custom fusion | bytes 1573376 | tf_op jit(solution)/shard_map/scatter | solution.py:45
  19.6 29.6 %all_to_all.15 = bf16[32,24,1024]{2,1,0:T(8,128)(2,1)S(1)} all-to-all(bf16[32,24,1024]{2,1,0:T(8,128)(2,1)S(1)} %bitcast.60), channel_id=1, replica_groups=mesh['dp'=16,'expert'=32] {'expert'}, dimensions={0} | all-to-all | bytes 3145728 | tf_op jit(solution)/shard_map/all_to_all | solution.py:47
  49.2 37.5 %all-gather.5.cloned.1.call-done = bf16[1,1024,704]{2,1,0:T(8,128)(2,1)} async-done(((bf16[1,64,704]{2,1,0:T(8,128)(2,1)}), bf16[1,1024,704]{2,1,0:T(8,128)(2,1)}) %all-gather.5.cloned.1.call-update) | async-done | bytes 1441808 | tf_op jit(solution)/shard_map/all_gather | solution.py:61
  86.7 4.1 fusion.2
  90.8 67.2 %all-gather.7.cloned.1.call-done = bf16[1,1024,704]{2,1,0:T(8,128)(2,1)} async-done(((bf16[1,64,704]{2,1,0:T(8,128)(2,1)}), bf16[1,1024,704]{2,1,0:T(8,128)(2,1)}) %all-gather.7.cloned.1.call-update) | async-done | bytes 1441808 | tf_op jit(solution)/shard_map/all_gather | solution.py:67
  158.0 4.7 convolution_convert_fusion
  162.7 7.6 %all-to-all-start.1 = ((bf16[32,24,1024]{2,1,0:T(8,128)(2,1)}), bf16[32,24,1024]{2,1,0:T(8,128)(2,1)S(1)}, u32[]{:S(2)}, u32[]{:S(2)}) async-start(bf16[32,24,1024]{2,1,0:T(8,128)(2,1)} %bitcast.8), calls=%async_computation.1 | async-start | bytes 3145728 | tf_op jit(solution)/shard_map/all_to_all | solution.py:71
  170.3 0.2 reduce-scatter.5.cloned.1.call-start
  170.5 0.7 copy.41
  171.3 0.6 fusion.29
  173.2 0.6 convert_reduce_fusion
  173.8 0.7 select_reduce_fusion.1
  174.5 15.9 %all-to-all-done.1 = bf16[32,24,1024]{2,1,0:T(8,128)(2,1)S(1)} async-done(((bf16[32,24,1024]{2,1,0:T(8,128)(2,1)}), bf16[32,24,1024]{2,1,0:T(8,128)(2,1)S(1)}, u32[]{:S(2)}, u32[]{:S(2)}) %all-to-all-start.1) | async-done | bytes 1572896 | tf_op jit(solution)/shard_map/all_to_all | solution.py:71
  190.4 2.8 gather_fusion
  193.2 1.8 reshape.174
  195.0 1.3 multiply_reduce_fusion
  196.4 0.2 multiply_reduce_fusion.2
  196.6 0.4 fusion.4
  197.0 31.4 %all_gather.15 = bf16[256,1024]{1,0:T(8,128)(2,1)S(1)} all-gather(bf16[16,1024]{1,0:T(8,128)(2,1)S(1)} %fusion.4), channel_id=1, replica_groups=mesh['dp'=16,'expert'=32] {'dp'}, dimensions={0}, use_global_device_ids=true | all-gather | bytes 557056 | tf_op jit(solution)/shard_map/all_gather | solution.py:96
  228.4 0.3 multiply_reduce_fusion.4
  228.7 27.0 %all-reduce.1 = f32[256]{0:T(256)S(1)} all-reduce(f32[256]{0:T(256)S(1)} %get-tuple-element.42), channel_id=4, replica_groups=mesh['dp'=16,'expert'=32] {'dp'}, use_global_device_ids=true, to_apply=%region_12.13.clone | all-reduce | flops 256 | bytes 2048
  255.8 0.1 select_reduce_fusion.4
  256.0 29.0 %all-reduce.3 = (f32[8]{0:T(128)S(1)}, f32[8]{0:T(128)S(1)}) all-reduce(f32[8]{0:T(128)S(1)} %get-tuple-element.28, f32[8]{0:T(128)S(1)} %get-tuple-element.27), channel_id=1, replica_groups=mesh['dp'=16,'expert'=32] {'dp'}, use_global_device_ids=true, to_apply=%region_9.10 | all-reduce | flops 16 | bytes 128 | tf_op jit(solution)/shard_map/psum | solution.py:114
  285.0 0.1 select_reduce_fusion.2
  285.1 0.1 subtract_dynamic-update-slice_fusion
  285.2 27.6 %all-reduce.2 = (f32[256]{0:T(256)S(1)}, f32[8]{0:T(128)}) all-reduce(f32[256]{0:T(256)S(1)} %subtract_dynamic-update-slice_fusion, f32[8]{0:T(128)S(1)} %get-tuple-element.25), channel_id=1, replica_groups=mesh['dp'=16,'expert'=32] {'dp'}, use_global_device_ids=true, to_apply=%add | all-reduce | flops 264 | bytes 2112
  312.8 1.2 convolution_convert_fusion.3
  314.0 0.1 mul.178
  314.1 64.8 %reduce-scatter.5.cloned.1.call-done = bf16[16,1024]{1,0:T(8,128)(2,1)} async-done(((bf16[256,1024]{1,0:T(8,128)(2,1)}), bf16[16,1024]{1,0:T(8,128)(2,1)}) %reduce-scatter.5.cloned.1.call-update) | async-done | bytes 32784 | tf_op jit(solution)/shard_map/reduce_scatter | solution.py:138
  378.9 1.3 multiply_reduce_fusion.1
  380.2 0.2 subtract_multiply_fusion
  380.4 1.9 mul.207
  382.3 2.0 mul.208
  384.3 3.9 scatter_custom_fusion.1
  388.2 7.5 %all-to-all-start.2 = ((bf16[32,24,1024]{2,1,0:T(8,128)(2,1)}), bf16[32,24,1024]{2,1,0:T(8,128)(2,1)S(1)}, u32[]{:S(2)}, u32[]{:S(2)}) async-start(bf16[32,24,1024]{2,1,0:T(8,128)(2,1)} %bitcast.59), calls=%async_computation.3 | async-start | bytes 3145728 | tf_op jit(solution)/shard_map/all_to_all | solution.py:159
  395.8 0.9 convolution_convert_fusion.4
  396.7 0.3 reduce-scatter.7.cloned.1.call-start
  397.0 18.9 %all-to-all-done.2 = bf16[32,24,1024]{2,1,0:T(8,128)(2,1)S(1)} async-done(((bf16[32,24,1024]{2,1,0:T(8,128)(2,1)}), bf16[32,24,1024]{2,1,0:T(8,128)(2,1)S(1)}, u32[]{:S(2)}, u32[]{:S(2)}) %all-to-all-start.2) | async-done | bytes 1572896 | tf_op jit(solution)/shard_map/all_to_all | solution.py:159
  415.9 4.2 convolution_convert_fusion.1
  420.0 6.6 %convolution_convert_fusion.2 = bf16[1024,704]{0,1:T(8,128)(2,1)} fusion(bf16[768,1024]{1,0:T(8,128)(2,1)S(1)} %bitcast.62, f32[768,704]{0,1:T(8,128)} %fusion.2, bf16[768,1024]{1,0:T(8,128)(2,1)S(1)} %bitcast.64, bf16[1,1024,704]{2,1,0:T(8,128)(2,1)} %all-gather.7.cloned.1.call-done), kind=kOutput, calls=%fused_computation.12 | convolution fusion | flops 2220179456 | bytes 8192000 | tf_op jit(solution)/shard_map/dot_general | solution.py:173
  426.6 2.1 pad_maximum_fusion
  428.7 2.9 copy.45
  431.6 0.1 multiply_reduce_fusion.3
  431.7 56.4 %psum.38 = bf16[64]{0:T(256)(128)(2,1)S(1)} all-reduce(bf16[64]{0:T(256)(128)(2,1)S(1)} %multiply_reduce_fusion.3), channel_id=1, replica_groups=mesh['dp'=16,'expert'=32] {'expert'}, use_global_device_ids=true, to_apply=%region_22.23 | all-reduce | flops 64 | bytes 256 | tf_op jit(solution)/shard_map/psum | solution.py:136
  488.1 0.5 convert_element_type.88
  488.6 0.6 subtract_reduce_fusion
  489.2 39.0 %all-reduce.6.cloned.1.call-done = bf16[64,1024]{1,0:T(8,128)(2,1)} async-done(((bf16[64,1024]{1,0:T(8,128)(2,1)}), bf16[64,1024]{1,0:T(8,128)(2,1)}) %all-reduce.6.cloned.1.call-update) | async-done | bytes 131088 | tf_op jit(solution)/shard_map/psum | solution.py:135
  528.2 1.6 convert_element_type.86
  529.8 76.8 %reduce-scatter.7.cloned.1.call-done = bf16[64,1408]{1,0:T(8,128)(2,1)} async-done(((bf16[1024,1408]{1,0:T(8,128)(2,1)}), bf16[64,1408]{1,0:T(8,128)(2,1)}) %reduce-scatter.7.cloned.1.call-update) | async-done | bytes 180240
  606.7 1.1 fusion.28
  607.8 0.2 copy.48
  607.9 0.8 copy.44
  608.7 0.2 copy.47
  608.9 0.8 copy.43
  (67 shorter events, 0.6 us)
Async XLA Ops:
  7.2 221.2 %copy-start = (bf16[64,1024]{1,0:T(8,128)(2,1)S(1)}, bf16[64,1024]{1,0:T(8,128)(2,1)}, u32[]{:S(2)}) copy-start(bf16[64,1024]{1,0:T(8,128)(2,1)} %param.18) | copy-start | bytes 393220
  7.2 79.5 %all-gather.5.cloned.1.call-start = ((), (), s32[]{:S(2)}) async-start(), calls=%async_computation.7 | async-start | bytes 1671168 | tf_op jit(solution)/shard_map/all_gather | solution.py:61
  7.9 150.1 %all-gather.7.cloned.1.call-start = ((), (), s32[]{:S(2)}) async-start(), calls=%async_computation.8 | async-start | bytes 1671168 | tf_op jit(solution)/shard_map/all_gather | solution.py:67
  49.2 41.6 %copy-start.2 = (bf16[32,24,1024]{2,1,0:T(8,128)(2,1)}, bf16[32,24,1024]{2,1,0:T(8,128)(2,1)S(1)}, u32[]{:S(2)}) copy-start(bf16[32,24,1024]{2,1,0:T(8,128)(2,1)S(1)} %all_to_all.15) | copy-start | bytes 4718596
  162.6 7.9 %copy-start.9 = (f32[128,4]{0,1:T(4,128)S(1)}, f32[128,4]{0,1:T(4,128)}, u32[]{:S(2)}) copy-start(f32[128,4]{0,1:T(4,128)} %param.15) | copy-start | bytes 6148
  162.6 8.6 %copy-start.16 = (u32[512]{0:T(512)S(1)}, u32[512]{0:T(512)}, u32[]{:S(2)}) copy-start(u32[512]{0:T(512)} %constant.64) | copy-start | bytes 6148
  162.6 10.5 %copy-start.12 = (s32[1,128]{1,0:T(1,128)S(1)}, s32[1,128]{1,0:T(1,128)}, u32[]{:S(2)}) copy-start(s32[1,128]{1,0:T(1,128)} %param.20) | copy-start | bytes 1540
  162.6 11.1 %copy-start.17 = (f32[32]{0:T(128)S(1)}, f32[32]{0:T(128)}, u32[]{:S(2)}) copy-start(f32[32]{0:T(128)} %param.25) | copy-start | bytes 388
  162.7 11.1 %copy-start.18 = (s32[1,16]{1,0:T(1,128)S(1)}, s32[1,16]{1,0:T(1,128)}, u32[]{:S(2)}) copy-start(s32[1,16]{1,0:T(1,128)} %param.23) | copy-start | bytes 196
  162.7 11.1 %copy-start.19 = (f32[32]{0:T(128)S(1)}, f32[32]{0:T(128)}, u32[]{:S(2)}) copy-start(f32[32]{0:T(128)} %param.24) | copy-start | bytes 388
  162.7 27.7 %all-to-all-start.1 = ((bf16[32,24,1024]{2,1,0:T(8,128)(2,1)}), bf16[32,24,1024]{2,1,0:T(8,128)(2,1)S(1)}, u32[]{:S(2)}, u32[]{:S(2)}) async-start(bf16[32,24,1024]{2,1,0:T(8,128)(2,1)} %bitcast.8), calls=%async_computation.1 | async-start | bytes 3145728 | tf_op jit(solution)/shard_map/all_to_all | solution.py:71
  170.3 208.6 %reduce-scatter.5.cloned.1.call-start = ((), (), s32[]{:S(2)}) async-start(), calls=%async_computation.5 | async-start | bytes 557056 | tf_op jit(solution)/shard_map/reduce_scatter | solution.py:138
  193.2 1.8 copy-start.6
  194.9 1.4 copy-start.1
  195.0 1.6 copy-start.14
  196.3 32.0 %copy-start.8 = (f32[64]{0:T(128)S(1)}, f32[64]{0:T(128)}, u32[]{:S(2)}) copy-start(f32[64]{0:T(128)} %param.19) | copy-start | bytes 772
  196.3 59.4 %copy-start.11 = (f32[16]{0:T(128)S(1)}, f32[16]{0:T(128)}, u32[]{:S(2)}) copy-start(f32[16]{0:T(128)} %get-tuple-element.30) | copy-start | bytes 196
  196.4 59.4 %copy-start.23 = (s32[1,16]{1,0:T(1,128)S(1)}, s32[1,16]{1,0:T(1,128)}, u32[]{:S(2)}) copy-start(s32[1,16]{1,0:T(1,128)} %param.22) | copy-start | bytes 196
  196.4 59.4 %copy-start.10 = (s32[1,16]{1,0:T(1,128)S(1)}, s32[1,16]{1,0:T(1,128)}, u32[]{:S(2)}) copy-start(s32[1,16]{1,0:T(1,128)} %param.21) | copy-start | bytes 196
  196.6 117.5 %copy-start.7 = (f32[128,4]{1,0:T(8,128)S(1)}, f32[128,4]{1,0:T(8,128)}, u32[]{:S(2)}) copy-start(f32[128,4]{1,0:T(8,128)} %copy.41) | copy-start | bytes 6148
  196.6 182.3 %copy-start.13 = (s32[1,128]{1,0:T(1,128)S(1)}, s32[1,128]{1,0:T(1,128)}, u32[]{:S(2)}) copy-start(s32[1,128]{1,0:T(1,128)} %param.20) | copy-start | bytes 1540
  196.6 182.3 %copy-start.15 = (f32[16]{0:T(128)S(1)}, f32[16]{0:T(128)}, u32[]{:S(2)}) copy-start(f32[16]{0:T(128)} %convert_reduce_fusion) | copy-start | bytes 196
  228.7 151.5 %copy-start.4 = (f32[256,64]{0,1:T(8,128)}, f32[256,64]{0,1:T(8,128)S(1)}, u32[]{:S(2)}) copy-start(f32[256,64]{0,1:T(8,128)S(1)} %get-tuple-element.43) | copy-start | bytes 196612
  285.0 95.4 %copy-start.20 = (f32[8]{0:T(128)}, f32[8]{0:T(128)S(1)}, u32[]{:S(2)}) copy-start(f32[8]{0:T(128)S(1)} %get-tuple-element.34) | copy-start | bytes 100
  388.2 7.6 %copy-start.5 = (f32[256,64]{0,1:T(8,128)S(1)}, f32[256,64]{0,1:T(8,128)}, u32[]{:S(2)}) copy-start(f32[256,64]{0,1:T(8,128)} %copy-done.4) | copy-start | bytes 196612
  388.2 27.7 %all-to-all-start.2 = ((bf16[32,24,1024]{2,1,0:T(8,128)(2,1)}), bf16[32,24,1024]{2,1,0:T(8,128)(2,1)S(1)}, u32[]{:S(2)}, u32[]{:S(2)}) async-start(bf16[32,24,1024]{2,1,0:T(8,128)(2,1)} %bitcast.59), calls=%async_computation.3 | async-start | bytes 3145728 | tf_op jit(solution)/shard_map/all_to_all | solution.py:159
  395.8 132.5 %all-reduce.6.cloned.1.call-start = ((), (), s32[]{:S(2)}) async-start(), calls=%async_computation.6 | async-start | bytes 262144 | tf_op jit(solution)/shard_map/psum | solution.py:135
  396.7 209.9 %reduce-scatter.7.cloned.1.call-start = ((), (), s32[]{:S(2)}) async-start(), calls=%async_computation.9 | async-start | bytes 3063808
  415.9 4.2 copy-start.3
  431.6 57.0 %copy-start.21 = (f32[8]{0:T(128)S(1)}, f32[8]{0:T(128)}, u32[]{:S(2)}) copy-start(f32[8]{0:T(128)} %copy-done.20) | copy-start | bytes 100
  431.6 57.0 %copy-start.22 = (f32[8]{0:T(128)S(1)}, f32[8]{0:T(128)}, u32[]{:S(2)}) copy-start(f32[8]{0:T(128)} %get-tuple-element.32) | copy-start | bytes 100
Sparse Core Ops, SparseCore 0:
  10.1 76.5 all-gather.4
  88.7 69.1 all-gather.6
  314.2 64.6 reduce-scatter.4
  400.4 127.7 all-reduce.5
  530.9 75.7 reduce-scatter.6
where the time goes:
time: 617 us; the launch traced here: 616 us
  waiting for transfers between devices  321 us (52%)
  blocking collectives  201 us (33%)
  local copies, waits for them, and re-layouts  24.7 us (4%)
  matrix products  23.6 us (4%)
  starting transfers between devices  15.7 us (3%)
  between operations  15.4 us (2%)
  other arithmetic  14.4 us (2%)
    unnamed x6, waiting for transfers between devices  78.3 us
    all_gather x1, waiting for transfers between devices, local(): lax.all_gather(down_local, 'dp', axis=0, tiled=True)  67.2 us
    reduce_scatter x1, waiting for transfers between devices, local(): lax.psum_scatter(jnp.dot(hid_grad, head_weight, preferred_element_type=jn...  64.8 us
    psum x1, blocking collectives, local(): lax.psum(out_term.astype(jnp.bfloat16), 'expert').astype(jnp.float32)  56.4 us
    unnamed x2, blocking collectives  54.6 us
    psum x1, waiting for transfers between devices, local(): lax.psum(head_term.astype(jnp.bfloat16), 'expert').astype(jnp.float32)  39 us
    all_gather x1, waiting for transfers between devices, local(): lax.all_gather(up_local, 'dp', axis=0, tiled=True)  37.5 us
    all_gather x1, blocking collectives, local(): all_pooled = lax.all_gather(pooled, 'dp', axis=0, tiled=True)  31.4 us
  transfers between devices with their start and end apart: 7, of which 7 were waited for; matrix products, arithmetic and copies ran while one was open for 6% of the time, Pallas kernels for 0%

commit v1 on v0

v1 whole, which is shorter than its diff:
```python
import functools

import jax
import jax.numpy as jnp
from jax import lax
from jax.experimental import pallas as pl
from jax.experimental.pallas import tpu as pltpu
from jax.sharding import PartitionSpec as P

LISTS = 8
RANKS = 32
MAIN = 16
OVER = 8
F32 = jnp.float32
BF16 = jnp.bfloat16
MESH = pl.DeviceIdType.MESH


def dot(a, b, ca=1, cb=0):
    return lax.dot_general(a, b, (((ca,), (cb,)), ((), ())), preferred_element_type=F32)


def iota(shape, dim):
    return lax.broadcasted_iota(jnp.int32, shape, dim)


def column(row, size):
    diagonal = iota((size, size), 0) == iota((size, size), 1)
    return jnp.sum(jnp.where(diagonal, jnp.broadcast_to(row, (size, size)), 0.0), axis=1, keepdims=True)


def split(value):
    high = value.astype(BF16)
    return high, (value - high.astype(F32)).astype(BF16)


def kernel(
    n_dp,
    n_exp,
    tok,
    ids,
    wts,
    up,
    down,
    head,
    out_w,
    pool,
    lists,
    clicks,
    ranks,
    alpha,
    beta,
    grad_up,
    grad_down,
    grad_head,
    grad_out,
    loss,
    snd1,
    rcv1,
    snd2,
    rcv2,
    snd3,
    rcv3,
    hot_main,
    hot_over,
    mix_main,
    mix_over,
    mix_main_t,
    mix_over_t,
    x_all,
    g_all,
    pre,
    act,
    pre_grad,
    up_all,
    down_all,
    head_all,
    ow_all,
    up_sum,
    down_sum,
    ring_buf,
    totals,
    hid_snd,
    hid_rcv,
    pooled_all,
    out_snd,
    out_rcv,
    head_term,
    piece_snd,
    piece_rcv,
    whole_piece,
    out_piece,
    a2a_send,
    a2a_recv,
    ring_send,
    ring_recv,
    dp_send,
    dp_recv,
    exp_send,
    exp_recv,
):
    toks, width = tok.shape
    top = ids.shape[1]
    half = width // 2
    cands = lists.shape[1]
    units = head.shape[0]
    hidden = units * n_dp
    group = min(16, n_exp)
    groups = n_exp // group
    g_main, g_over = group * MAIN, group * OVER
    g_rows = g_main + g_over
    me_d = lax.axis_index("dp")
    me_e = lax.axis_index("expert")
    right = lax.rem(me_d + 1, n_dp)
    left = lax.rem(me_d + n_dp - 1, n_dp)

    def over_peers(axis, size, me, do):
        def body(k, carry):
            do(lax.rem(me + k, size))
            return carry

        lax.fori_loop(1, size, body, 0)

    def expert_peers(do):
        over_peers("expert", n_exp, me_e, do)

    def dp_peers(do):
        over_peers("dp", n_dp, me_d, do)

    def remote(src, dst, send, recv, axis, peer):
        return pltpu.make_async_remote_copy(
            src_ref=src,
            dst_ref=dst,
            send_sem=send,
            recv_sem=recv,
            device_id={axis: peer},
            device_id_type=MESH,
        )

    def exchange(n, src, dst, p):
        return remote(src.at[p], dst.at[me_e], a2a_send.at[n, p], a2a_recv.at[n, me_e], "expert", p)

    def arrived(n, src, dst, p):
        remote(src.at[p], dst.at[p], a2a_send.at[n, p], a2a_recv.at[n, p], "expert", p).wait_recv()

    def send_group(n, src, dst, g):
        def body(k, carry):
            p = g * group + lax.rem(me_e + k, group)

            @pl.when(p != me_e)
            def _():
                exchange(n, src, dst, p).start()

            return carry

        lax.fori_loop(0, group, body, 0)

    def keep_own(src, dst):
        dst[pl.ds(me_e, 1)] = src[pl.ds(me_e, 1)]

    def pack(dst, g, main, over):
        peers = pl.ds(g * group, group)
        dst[peers, :, 0:width] = main.astype(BF16).reshape(group, MAIN, width)
        low = over[:, 0:half].reshape(group, OVER, half)
        high = over[:, half:width].reshape(group, OVER, half)
        dst[peers, :, width : width + half] = jnp.concatenate([low, high], axis=1).astype(BF16)

    def unpack(src, g):
        peers = pl.ds(g * group, group)
        main = src[peers, :, 0:width].reshape(g_main, width)
        both = src[peers, :, width : width + half].astype(F32)
        low = both[:, 0:OVER, :].reshape(g_over, half)
        high = both[:, OVER : 2 * OVER, :].reshape(g_over, half)
        return main, jnp.concatenate([low, high], axis=1).astype(BF16)

    with jax.named_scope("greet"):
        barrier = pltpu.get_barrier_semaphore()
        expert_peers(
            lambda p: pl.semaphore_signal(barrier, inc=1, device_id={"expert": p}, device_id_type=MESH)
        )
        dp_peers(lambda p: pl.semaphore_signal(barrier, inc=1, device_id={"dp": p}, device_id_type=MESH))

    with jax.named_scope("slots"):
        up_all[pl.ds(me_d, 1)] = up[...]
        down_all[pl.ds(me_d, 1)] = down[...]
        head_all[pl.ds(me_d, 1)] = head[...].reshape(1, units, width)
        lane = iota((toks, 128), 1)
        named = jnp.zeros((toks, 128), F32)
        weight = jnp.zeros((toks, 128), F32)
        for k in range(top):
            hit = ids[:, k : k + 1] == lane
            named = jnp.where(hit, 1.0, named)
            weight = jnp.where(hit, wts[:, k : k + 1], weight)
        named_t = jnp.transpose(named)[0:n_exp]
        weight_t = jnp.transpose(weight)[0:n_exp]
        earlier = jnp.where(iota((toks, toks), 0) < iota((toks, toks), 1), 1.0, 0.0).astype(BF16)
        slot_t = jnp.where(named_t > 0.5, dot(named_t.astype(BF16), earlier), -1.0)

        def one_hot(first, rows):
            slot = (iota((n_exp, rows, toks), 1) + first).astype(F32)
            return jnp.where(slot_t[:, None, :] == slot, 1.0, 0.0).reshape(n_exp * rows, toks)

        hot_main[...] = one_hot(0, MAIN).astype(BF16)
        hot_over[...] = one_hot(MAIN, OVER).astype(BF16)

        def dispatch(g, carry):
            pack(
                snd1,
                g,
                dot(hot_main[pl.ds(g * g_main, g_main), :], tok[...]),
                dot(hot_over[pl.ds(g * g_over, g_over), :], tok[...]),
            )
            return carry

        lax.fori_loop(0, groups, dispatch, 0)
        parity = lax.rem(me_d, 2)
        own_half = iota((8, 128), 1) // units == parity
        ow_all[pl.ds(me_d, 1)] = jnp.where(own_half, jnp.broadcast_to(out_w[...], (8, 128)), 0.0).reshape(1, 8, 128)
        keep_own(snd1, rcv1)

    with jax.named_scope("barrier_wait"):
        pl.semaphore_wait(barrier, n_exp - 1 + n_dp - 1)

    far = n_dp // 2
    near = n_dp - 1 - far

    def hop(chain, step):
        buf, rows, to_right, steps, sem = chain
        owner = lax.rem(me_d + (n_dp - step if to_right else step), n_dp)
        place = buf.at[owner, rows]
        return remote(
            place, place, ring_send.at[sem, step], ring_recv.at[sem, step], "dp", right if to_right else left
        )

    def came(chain, step):
        buf, rows, to_right, steps, sem = chain
        owner = lax.rem(me_d + (n_dp - 1 - step if to_right else step + 1), n_dp)
        place = buf.at[owner, rows]
        remote(
            place, place, ring_send.at[sem, step], ring_recv.at[sem, step], "dp", right if to_right else left
        ).wait_recv()

    def ring_start(chains):
        for chain in chains:
            hop(chain, 0).start()

    def ring_rest(chains):
        def body(step, carry):
            for chain in chains:
                steps = chain[3]

                @pl.when(step < steps)
                def _(chain=chain, steps=steps):
                    came(chain, step)

                    @pl.when(step + 1 < steps)
                    def _():
                        hop(chain, step + 1).start()

            return carry

        lax.fori_loop(0, far, body, 0)

    def ring_drain(chains):
        for chain in chains:

            def body(step, carry, chain=chain):
                hop(chain, step).wait_send()
                return carry

            lax.fori_loop(0, chain[3], body, 0)

    all_rows = pl.ds(0, units)
    first_rows = pl.ds(0, units // 2)
    last_rows = pl.ds(units // 2, units // 2)
    weight_chains = [
        (up_all, all_rows, True, far, 0),
        (up_all, all_rows, False, near, 1),
        (down_all, all_rows, True, near, 2),
        (down_all, all_rows, False, far, 3),
    ]
    head_chains = [
        (head_all, first_rows, True, far, 4),
        (head_all, first_rows, False, near, 5),
        (head_all, last_rows, True, near, 6),
        (head_all, last_rows, False, far, 7),
    ]

    def push(n, src, dst, p):
        return remote(src, dst.at[me_d], dp_send.at[n, p], dp_recv.at[n, me_d], "dp", p)

    def pushed(n, src, dst, p):
        remote(src, dst.at[p], dp_send.at[n, p], dp_recv.at[n, p], "dp", p).wait_recv()

    with jax.named_scope("dispatch_send"):
        ring_start(weight_chains)
        for g in range(groups):
            send_group(0, snd1, rcv1, g)
        dp_peers(lambda p: push(0, ow_all.at[me_d], ow_all, p).start())

    with jax.named_scope("mix_tables"):
        weight_high, weight_low = split(weight_t)

        def spread(part, hot, rows):
            wide = jnp.broadcast_to(part.astype(F32)[:, None, :], (n_exp, rows, toks))
            return hot[...].astype(F32) * wide.reshape(n_exp * rows, toks)

        def both(hot, rows):
            return jnp.concatenate(
                [spread(weight_high, hot, rows), spread(weight_low, hot, rows)], axis=1
            )

        table = both(hot_main, MAIN)
        mix_main[...] = table.astype(BF16)
        mix_main_t[...] = jnp.transpose(table).astype(BF16)
        table = both(hot_over, OVER)
        mix_over[...] = table.astype(BF16)
        mix_over_t[...] = jnp.transpose(table).astype(BF16)

    with jax.named_scope("weight_ring"):
        ring_rest(weight_chains)

    with jax.named_scope("dispatch_wait"):
        expert_peers(lambda p: arrived(0, snd1, rcv1, p))

    with jax.named_scope("expert_forward"):
        ring_start(head_chains)

        def forward(g, carry):
            main, over = unpack(rcv1, g)
            rows = pl.ds(pl.multiple_of(g * g_rows, 16), g_rows)
            x = jnp.concatenate([main, over], axis=0)
            x_all[rows, :] = x
            up_full = up_all[...].reshape(width, up.shape[2])
            pre_act = dot(x, up_full)
            pre[rows, :] = pre_act
            activated = (pre_act * jax.nn.sigmoid(pre_act)).astype(BF16)
            act[rows, :] = activated
            out = dot(activated, down_all[...].reshape(width, down.shape[2]), 1, 1)
            pack(snd2, g, out[0:g_main], out[g_main:g_rows])
            send_group(1, snd2, rcv2, g)
            return carry

        lax.fori_loop(0, groups, forward, 0)
        keep_own(snd2, rcv2)

    with jax.named_scope("head_ring"):
        ring_rest(head_chains)

    with jax.named_scope("slope"):

        def slope(g, carry):
            rows = pl.ds(pl.multiple_of(g * (g_rows // 4), 16), g_rows // 4)
            pre_act = pre[rows, :]
            sigmoid = jax.nn.sigmoid(pre_act)
            pre[rows, :] = sigmoid * (1.0 + pre_act * (1.0 - sigmoid))
            return carry

        lax.fori_loop(0, groups * 4, slope, 0)
        pool_row = pool[...].astype(F32)
        member_t = jnp.where(iota((cands, toks), 0).astype(F32) == pool_row, 1.0, 0.0)
        counts = jnp.sum(member_t, axis=1, keepdims=True)
        pool_column = column(pool_row, toks)
        member = jnp.where(iota((toks, cands), 1).astype(F32) == pool_column, 1.0, 0.0).astype(BF16)
        member_t = member_t.astype(BF16)
        list_hot = jnp.where(
            iota((cands, 128), 1).astype(F32) == column(lists[...].astype(F32), cands), 1.0, 0.0
        )
        rank_hot = jnp.where(
            iota((cands, RANKS), 1).astype(F32) == column(ranks[...].astype(F32), cands), 1.0, 0.0
        )
        alpha_of = jnp.sum(rank_hot * alpha[...], axis=1, keepdims=True)
        beta_of = jnp.sum(rank_hot * beta[...], axis=1, keepdims=True)
        corrected = (column(clicks[...].astype(F32), cands) - beta_of) / alpha_of
        dp_peers(lambda p: pushed(0, ow_all.at[me_d], ow_all, p))
        ow_row = jnp.concatenate(
            [(ow_all[2 * k] + ow_all[2 * k + 1])[0:1] for k in range(hidden // 128)], axis=1
        )

    with jax.named_scope("return_wait"):
        expert_peers(lambda p: arrived(1, snd2, rcv2, p))

    with jax.named_scope("mix"):
        stacked = jnp.zeros((2 * toks, width), F32)
        for g in range(groups):
            main, over = unpack(rcv2, g)
            stacked = stacked + dot(mix_main_t[:, g * g_main : (g + 1) * g_main], main)
            stacked = stacked + dot(mix_over_t[:, g * g_over : (g + 1) * g_over], over)
        mixed = tok[...].astype(F32) + (stacked[0:toks] + stacked[toks : 2 * toks])
        inv_rms = lax.rsqrt(jnp.mean(mixed * mixed, axis=1, keepdims=True) + 1e-06)
        normed = mixed * inv_rms
        normed_high, normed_low = split(normed)
        pooled_sum = dot(member_t, normed_high) + dot(member_t, normed_low)
        pooled = (pooled_sum / counts).astype(BF16)
    with jax.named_scope("head_forward"):
        head_act = jnp.tanh(dot(pooled, head_all[...].reshape(hidden, width), 1, 1))
        scores = jnp.sum(head_act * ow_row, axis=1, keepdims=True)
        exp_scores = jnp.exp(scores)
        tile_row = iota((8, 128), 0)
        terms = jnp.zeros((8, 128), F32)
        for k, value in enumerate((exp_scores, corrected, corrected * scores)):
            terms = jnp.where(tile_row == k, jnp.sum(value * list_hot, axis=0, keepdims=True), terms)
        totals[pl.ds(me_d, 1)] = terms.reshape(1, 8, 128)
    with jax.named_scope("totals"):
        dp_peers(lambda p: push(1, totals.at[me_d], totals, p).start())
        dp_peers(lambda p: pushed(1, totals.at[me_d], totals, p))
    with jax.named_scope("head_backward"):
        total = jnp.sum(totals[...], axis=0)
        in_list = iota((1, 128), 1) < LISTS
        exp_total = jnp.where(in_list, total[0:1], 1.0)
        click_total = jnp.where(in_list, total[1:2], 0.0)
        cross_total = jnp.where(in_list, total[2:3], 0.0)
        loss[...] = jnp.sum(click_total * jnp.log(exp_total) - cross_total, axis=1, keepdims=True)
        ratio = jnp.sum(list_hot * (click_total / exp_total), axis=1, keepdims=True)
        cand_grad = ratio * exp_scores - corrected
        hid_grad = (cand_grad * ow_row * (1.0 - head_act * head_act)).astype(BF16)
        pooled_grad = dot(hid_grad, head_all[...].reshape(hidden, width)) / counts
        grad_high, grad_low = split(pooled_grad)
        normed_grad = dot(member, grad_high) + dot(member, grad_low)
        mixed_grad = inv_rms * (normed_grad - normed * jnp.mean(normed_grad * normed, axis=1, keepdims=True))
        once = mixed_grad.astype(BF16)
        twice = jnp.concatenate([once, once], axis=0)
    with jax.named_scope("grad_send"):
        for g in range(groups):
            pack(
                snd3,
                g,
                dot(mix_main[g * g_main : (g + 1) * g_main, :], twice),
                dot(mix_over[g * g_over : (g + 1) * g_over, :], twice),
            )
            send_group(2, snd3, rcv3, g)
        keep_own(snd3, rcv3)

        out_term = jnp.sum(cand_grad * head_act, axis=0, keepdims=True)
        for k in range(hidden // 128):
            hid_snd[k] = hid_grad[:, k * 128 : (k + 1) * 128]
            out_snd[k] = jnp.broadcast_to(out_term[:, k * 128 : (k + 1) * 128], (8, 128))
        pooled_all[pl.ds(me_d, 1)] = pooled.reshape(1, cands, width)
        hid_rcv[pl.ds(me_d, 1)] = hid_snd[pl.ds(me_d // 2, 1)]
        out_rcv[pl.ds(me_d, 1)] = out_snd[pl.ds(me_d // 2, 1)]

        def send_terms(p):
            push(2, hid_snd.at[p // 2], hid_rcv, p).start()
            push(3, out_snd.at[p // 2], out_rcv, p).start()
            push(4, pooled_all.at[me_d], pooled_all, p).start()

        dp_peers(send_terms)

    with jax.named_scope("grad_wait"):
        expert_peers(lambda p: arrived(2, snd3, rcv3, p))

    tile = min(256, width)
    blocks = tile // units

    def term(dst, a, b):
        def body(f, carry):
            part = dot(a[:, pl.ds(pl.multiple_of(f * tile, 128), tile)], b[...], 0, 0)
            dst[pl.ds(f * blocks, blocks)] = part.astype(BF16).reshape(blocks, units, b.shape[1])
            return carry

        lax.fori_loop(0, width // tile, body, 0)

    def sum_hop(chain, step):
        own, to_right, steps, sem, slot = chain
        if isinstance(step, int) and step == 0:
            owner = lax.rem(me_d + (steps if to_right else n_dp - steps), n_dp)
            src = own.at[owner]
        else:
            src = ring_buf.at[slot, step - 1]
        return remote(
            src,
            ring_buf.at[slot, step],
            ring_send.at[sem, step],
            ring_recv.at[sem, step],
            "dp",
            right if to_right else left,
        )

    def sum_came(chain, step):
        own, to_right, steps, sem, slot = chain
        place = ring_buf.at[slot, step]
        remote(
            place, place, ring_send.at[sem, step], ring_recv.at[sem, step], "dp", right if to_right else left
        ).wait_recv()

    up_chains = [(up_sum, True, far, 8, 0), (up_sum, False, near, 9, 1)]
    down_chains = [(down_sum, True, near, 10, 2), (down_sum, False, far, 11, 3)]

    with jax.named_scope("down_term"):

        def gather(g, carry):
            main, over = unpack(rcv3, g)
            rows = pl.ds(pl.multiple_of(g * g_rows, 16), g_rows)
            g_all[rows, :] = jnp.concatenate([main, over], axis=0)
            return carry

        lax.fori_loop(0, groups, gather, 0)
        term(down_sum, g_all, act)
        for chain in down_chains:
            sum_hop(chain, 0).start()

    with jax.named_scope("up_term"):

        def backward(g, carry):
            rows = pl.ds(pl.multiple_of(g * g_rows, 16), g_rows)
            act_grad = dot(g_all[rows, :], down_all[...].reshape(width, down.shape[2]))
            pre_grad[rows, :] = (act_grad * pre[rows, :]).astype(BF16)
            return carry

        lax.fori_loop(0, groups, backward, 0)
        term(up_sum, x_all, pre_grad)
        for chain in up_chains:
            sum_hop(chain, 0).start()

    columns = width // 128
    with jax.named_scope("head_term"):

        def got_terms(p):
            pushed(2, hid_snd.at[p // 2], hid_rcv, p)
            pushed(3, out_snd.at[p // 2], out_rcv, p)
            pushed(4, pooled_all.at[me_d], pooled_all, p)

        dp_peers(got_terms)
        head_term[...] = dot(
            hid_rcv[...].reshape(n_dp * cands, 128), pooled_all[...].reshape(n_dp * cands, width), 0, 0
        )
        mine = head_term[pl.ds(pl.multiple_of(parity * units, 8), units), :].astype(BF16)
        for q in range(n_exp):
            a, b = q // columns, q % columns
            piece_snd[q] = mine[a * 16 : (a + 1) * 16, b * 128 : (b + 1) * 128]
        piece_rcv[pl.ds(me_e, 1)] = piece_snd[pl.ds(me_e, 1)]
        out_piece[pl.ds(me_e, 1)] = jnp.sum(out_rcv[...], axis=0).reshape(1, 8, 128)

    def piece(p):
        return remote(piece_snd.at[p], piece_rcv.at[me_e], exp_send.at[0, p], exp_recv.at[0, me_e], "expert", p)

    def out_push(p):
        return remote(out_piece.at[me_e], out_piece.at[me_e], exp_send.at[1, p], exp_recv.at[1, me_e], "expert", p)

    def whole_push(p):
        return remote(whole_piece.at[me_e], whole_piece.at[me_e], exp_send.at[2, p], exp_recv.at[2, me_e], "expert", p)

    def got(n, ref, p):
        remote(ref.at[p], ref.at[p], exp_send.at[n, p], exp_recv.at[n, p], "expert", p).wait_recv()

    def send_pieces(p):
        piece(p).start()
        out_push(p).start()

    expert_peers(send_pieces)

    def sum_steps(first, last):
        def body(step, carry):
            for chain in down_chains + up_chains:
                own, to_right, steps, sem, slot = chain

                @pl.when(step + 1 < steps)
                def _(chain=chain):
                    own, to_right, steps, sem, slot = chain
                    sum_came(chain, step)
                    owner = lax.rem(
                        me_d + (steps - 1 - step if to_right else n_dp - (steps - 1) + step), n_dp
                    )
                    total = ring_buf[slot, pl.ds(step, 1)].astype(F32) + own[pl.ds(owner, 1)].astype(F32)
                    ring_buf[slot, pl.ds(step, 1)] = total.astype(BF16)
                    sum_hop(chain, step + 1).start()

            return carry

        lax.fori_loop(first, last, body, 0)

    with jax.named_scope("sum_ring_first"):
        middle = min(3, far - 1)
        sum_steps(0, middle)

    with jax.named_scope("head_pieces"):
        expert_peers(lambda p: got(0, piece_rcv, p))
        whole_piece[pl.ds(me_e, 1)] = jnp.sum(piece_rcv[...].astype(F32), axis=0).reshape(1, 16, 128)
        expert_peers(lambda p: whole_push(p).start())

    with jax.named_scope("sum_ring_last"):
        sum_steps(middle, far - 1)

    with jax.named_scope("head_out"):
        expert_peers(lambda p: got(1, out_piece, p))
        out_all = jnp.sum(out_piece[...], axis=0)[0:1]
        out_pair = jnp.where(parity == 0, out_all, pltpu.roll(out_all, 128 - units, 1))
        grad_out[...] = out_pair[:, 0:units]
        expert_peers(lambda p: got(2, whole_piece, p))
        for q in range(n_exp):
            a, b = q // columns, q % columns
            grad_head[a * 16 : (a + 1) * 16, b * 128 : (b + 1) * 128] = whole_piece[q]

    with jax.named_scope("sum_end"):
        for dst, chains in ((grad_down, down_chains), (grad_up, up_chains)):
            total = chains[0][0][pl.ds(me_d, 1)].astype(F32)
            for chain in chains:
                own, to_right, steps, sem, slot = chain
                sum_came(chain, steps - 1)
                total = total + ring_buf[slot, steps - 1].astype(F32)[None]
            dst[...] = total.astype(BF16)

    with jax.named_scope("drain"):

        def drain_expert(p):
            exchange(0, snd1, rcv1, p).wait_send()
            exchange(1, snd2, rcv2, p).wait_send()
            exchange(2, snd3, rcv3, p).wait_send()
            piece(p).wait_send()
            out_push(p).wait_send()
            whole_push(p).wait_send()

        expert_peers(drain_expert)

        def drain_dp(p):
            push(0, ow_all.at[me_d], ow_all, p).wait_send()
            push(1, totals.at[me_d], totals, p).wait_send()
            push(2, hid_snd.at[p // 2], hid_rcv, p).wait_send()
            push(3, out_snd.at[p // 2], out_rcv, p).wait_send()
            push(4, pooled_all.at[me_d], pooled_all, p).wait_send()

        dp_peers(drain_dp)
        ring_drain(weight_chains + head_chains)
        for chain in down_chains + up_chains:
            sum_hop(chain, 0).wait_send()

            def body(step, carry, chain=chain):
                sum_hop(chain, step).wait_send()
                return carry

            lax.fori_loop(1, chain[2], body, 0)


def local(
    tokens,
    route_ids,
    route_weights,
    up_weight,
    down_weight,
    head_weight,
    out_weight,
    pool_ids,
    list_ids,
    clicks,
    ranks,
    alpha_table,
    beta_table,
):
    n_dp = lax.axis_size("dp")
    n_exp = lax.axis_size("expert")
    toks, width = tokens.shape
    ff = up_weight.shape[2]
    units = head_weight.shape[0]
    cands = list_ids.shape[1]
    slots = n_exp * (MAIN + OVER)
    wire = pltpu.VMEM((n_exp, MAIN, width + width // 2), BF16)
    steps = n_dp // 2
    pairs = units * n_dp // 128
    vmem = pl.BlockSpec(memory_space=pltpu.VMEM)
    outs = pl.pallas_call(
        functools.partial(kernel, n_dp, n_exp),
        out_shape=(
            jax.ShapeDtypeStruct(up_weight.shape, BF16),
            jax.ShapeDtypeStruct(down_weight.shape, BF16),
            jax.ShapeDtypeStruct(head_weight.shape, F32),
            jax.ShapeDtypeStruct((1, units), F32),
            jax.ShapeDtypeStruct((1, 1), F32),
        ),
        in_specs=[vmem] * 13,
        out_specs=(vmem,) * 5,
        scratch_shapes=[
            wire,
            wire,
            wire,
            wire,
            wire,
            wire,
            pltpu.VMEM((n_exp * MAIN, toks), BF16),
            pltpu.VMEM((n_exp * OVER, toks), BF16),
            pltpu.VMEM((n_exp * MAIN, 2 * toks), BF16),
            pltpu.VMEM((n_exp * OVER, 2 * toks), BF16),
            pltpu.VMEM((2 * toks, n_exp * MAIN), BF16),
            pltpu.VMEM((2 * toks, n_exp * OVER), BF16),
            pltpu.VMEM((slots, width), BF16),
            pltpu.VMEM((slots, width), BF16),
            pltpu.VMEM((slots, ff), F32),
            pltpu.VMEM((slots, ff), BF16),
            pltpu.VMEM((slots, ff), BF16),
            pltpu.VMEM((n_dp, width // n_dp, ff), BF16),
            pltpu.VMEM((n_dp, width // n_dp, ff), BF16),
            pltpu.VMEM((n_dp, units, width), BF16),
            pltpu.VMEM((n_dp, 8, 128), F32),
            pltpu.VMEM((n_dp, width // n_dp, ff), BF16),
            pltpu.VMEM((n_dp, width // n_dp, ff), BF16),
            pltpu.VMEM((4, steps, width // n_dp, ff), BF16),
            pltpu.VMEM((n_dp, 8, 128), F32),
            pltpu.VMEM((pairs, cands, 128), BF16),
            pltpu.VMEM((n_dp, cands, 128), BF16),
            pltpu.VMEM((n_dp, cands, width), BF16),
            pltpu.VMEM((pairs, 8, 128), F32),
            pltpu.VMEM((n_dp, 8, 128), F32),
            pltpu.VMEM((128, width), F32),
            pltpu.VMEM((n_exp, 16, 128), BF16),
            pltpu.VMEM((n_exp, 16, 128), BF16),
            pltpu.VMEM((n_exp, 16, 128), F32),
            pltpu.VMEM((n_exp, 8, 128), F32),
            pltpu.SemaphoreType.DMA((3, n_exp)),
            pltpu.SemaphoreType.DMA((3, n_exp)),
            pltpu.SemaphoreType.DMA((12, steps)),
            pltpu.SemaphoreType.DMA((12, steps)),
            pltpu.SemaphoreType.DMA((5, n_dp)),
            pltpu.SemaphoreType.DMA((5, n_dp)),
            pltpu.SemaphoreType.DMA((3, n_exp)),
            pltpu.SemaphoreType.DMA((3, n_exp)),
        ],
        compiler_params=pltpu.CompilerParams(
            collective_id=0, has_side_effects=True, vmem_limit_bytes=56 * 1024 * 1024
        ),
    )(
        tokens,
        route_ids,
        route_weights,
        up_weight,
        down_weight,
        head_weight,
        jnp.concatenate([out_weight, out_weight]).reshape(1, 2 * units),
        pool_ids,
        list_ids,
        clicks,
        ranks,
        alpha_table.reshape(1, RANKS),
        beta_table.reshape(1, RANKS),
    )
    grad_up, grad_down, grad_head, grad_out, list_loss = outs
    return grad_up, grad_down, grad_head, grad_out.reshape(units), list_loss.reshape(1)


def solution(mesh):
    return jax.shard_map(
        local,
        mesh=mesh,
        in_specs=(
            P(("dp", "expert"), None),
            P(("dp", "expert"), None),
            P(("dp", "expert"), None),
            P("expert", "dp", None),
            P("expert", "dp", None),
            P("dp", None),
            P("dp"),
            P(("dp", "expert"), None),
            P(("dp", "expert"), None),
            P(("dp", "expert"), None),
            P(("dp", "expert"), None),
            P(),
            P(),
        ),
        out_specs=(
            P("expert", "dp", None),
            P("expert", "dp", None),
            P("dp", None),
            P("dp"),
            P("expert"),
        ),
        check_vma=False,
    )
```

time: 617 us -> 181 us (0.29)
  the two profiles are of different devices: /device:TPU:2 before, /device:TPU:28 now
where the time goes in v1:
time: 181 us
  Pallas kernels  172 us (95%)
  local copies, waits for them, and re-layouts  6.47 us (4%)
  between operations  2.41 us (1%)
    pallas_call x1, Pallas kernels, local(): pl.pallas_call(functools.partial(kernel, n_dp, n_exp), out_shape=(jax.Sha...  172 us
    unnamed x16, local copies, waits for them, and re-layouts  6.47 us

profile of v1, /device:TPU:28, one launch (start us, length us, event | category | flops | bytes accessed | tf_op | source)
XLA Modules:
  0.0 181.1 jit_solution(12145145483577712713)
XLA Ops:
  0.6 0.0 copy-start.3
  0.6 0.0 copy-start.1
  0.7 0.6 copy-done.3
  1.3 0.6 maximum_bitcast_fusion.out_w
  1.9 0.0 copy-done.1
  1.9 0.0 copy-start.2
  1.9 0.7 copy.18.ids
  2.6 0.0 copy-done.2
  2.6 0.7 copy.19.wts
  3.4 171.6 %shard_map.164 = (bf16[1,64,704]{2,1,0:T(8,128)(2,1)}, bf16[1,64,704]{2,1,0:T(8,128)(2,1)}, f32[64,1024]{1,0:T(8,128)}, f32[1,64]{1,0:T(1,128)}, f32[1,1]{1,0:T(1,128)}) custom-call(bf16[128,1024]{1,0:T(8,128)(2,1)} %tok.1, s32[128,4]{1,0:T(8,128)} %copy.18.ids, f32[128,4]{1,0:T(8,128)} %copy.19.wts, bf16[1,64,704]{2,1,0:T(8,128)(2,1)} %up.1, ...), custom_call_target="tpu_custom_call" | custom-call | tf_op jit(solution)/shard_map/pallas_call | solution.py:660
  175.0 0.0 copy-start
  175.0 1.6 copy.25
  176.6 1.5 copy.26
  178.1 0.0 copy-done
  178.1 0.0 copy-start.4
  178.1 0.7 copy.27
  178.8 0.0 copy-done.4
  178.8 0.5 copy.28
Async XLA Ops:
  0.6 0.7 copy-start.3
  0.6 1.2 copy-start.1
  1.9 0.7 copy-start.2
  175.0 3.1 %copy-start = (f32[64,1024]{1,0:T(8,128)S(1)}, f32[64,1024]{1,0:T(8,128)}, u32[]{:S(2)}) copy-start(f32[64,1024]{1,0:T(8,128)} %get-tuple-element.22) | copy-start | bytes 786436
  178.1 0.7 copy-start.4

commit v2 on v1

--- a/solution.py
+++ b/solution.py
@@ -72,13 +72,15 @@
     pre,
     act,
     pre_grad,
-    up_all,
-    down_all,
+    wide_all,
+    rest_all,
+    down_full,
     head_all,
     ow_all,
     up_sum,
     down_sum,
-    ring_buf,
+    up_ring,
+    down_ring,
     totals,
     hid_snd,
     hid_rcv,
@@ -98,9 +100,15 @@
     dp_recv,
     exp_send,
     exp_recv,
+    twin_send,
+    twin_recv,
 ):
     toks, width = tok.shape
-    top = ids.shape[1]
+    top = ids.shape[0]
+    ff = up.shape[2]
+    lanes = wide_all.shape[2]
+    spare = lanes - ff
+    rest = rest_all.shape[2]
     half = width // 2
     cands = lists.shape[1]
     units = head.shape[0]
@@ -181,18 +189,20 @@
         dp_peers(lambda p: pl.semaphore_signal(barrier, inc=1, device_id={"dp": p}, device_id_type=MESH))
 
     with jax.named_scope("slots"):
-        up_all[pl.ds(me_d, 1)] = up[...]
-        down_all[pl.ds(me_d, 1)] = down[...]
+        pad = jnp.zeros((up.shape[1], spare), F32)
+        turned = pltpu.roll(jnp.concatenate([down[0].astype(F32), pad], axis=1), lanes - spare, 1)
+        up_wide = jnp.concatenate([up[0].astype(F32), pad], axis=1)
+        own_wide = jnp.where(iota((up.shape[1], lanes), 1) < ff, up_wide, turned)
+        wide_all[pl.ds(me_d, 1)] = own_wide.astype(BF16)[None]
+        rest_all[pl.ds(me_d, 1)] = turned[:, 0:rest].astype(BF16)[None]
         head_all[pl.ds(me_d, 1)] = head[...].reshape(1, units, width)
-        lane = iota((toks, 128), 1)
-        named = jnp.zeros((toks, 128), F32)
-        weight = jnp.zeros((toks, 128), F32)
+        expert = iota((n_exp, toks), 0)
+        named_t = jnp.zeros((n_exp, toks), F32)
+        weight_t = jnp.zeros((n_exp, toks), F32)
         for k in range(top):
-            hit = ids[:, k : k + 1] == lane
-            named = jnp.where(hit, 1.0, named)
-            weight = jnp.where(hit, wts[:, k : k + 1], weight)
-        named_t = jnp.transpose(named)[0:n_exp]
-        weight_t = jnp.transpose(weight)[0:n_exp]
+            hit = ids[k : k + 1, :] == expert
+            named_t = jnp.where(hit, 1.0, named_t)
+            weight_t = jnp.where(hit, wts[k : k + 1, :], weight_t)
         earlier = jnp.where(iota((toks, toks), 0) < iota((toks, toks), 1), 1.0, 0.0).astype(BF16)
         slot_t = jnp.where(named_t > 0.5, dot(named_t.astype(BF16), earlier), -1.0)
 
@@ -214,8 +224,9 @@
 
         lax.fori_loop(0, groups, dispatch, 0)
         parity = lax.rem(me_d, 2)
-        own_half = iota((8, 128), 1) // units == parity
-        ow_all[pl.ds(me_d, 1)] = jnp.where(own_half, jnp.broadcast_to(out_w[...], (8, 128)), 0.0).reshape(1, 8, 128)
+        own_row = jnp.concatenate([out_w[...], jnp.zeros((1, 128 - units), F32)], axis=1)
+        own_row = jnp.where(parity == 0, own_row, pltpu.roll(own_row, units, 1))
+        ow_all[pl.ds(me_d, 1)] = jnp.broadcast_to(own_row, (8, 128))[None]
         keep_own(snd1, rcv1)
 
     with jax.named_scope("barrier_wait"):
@@ -244,22 +255,28 @@
         for chain in chains:
             hop(chain, 0).start()
 
-    def ring_rest(chains):
+    def ring_step(chains, step, each):
+        for chain in chains:
+            steps = chain[3]
+
+            @pl.when(step < steps)
+            def _(chain=chain, steps=steps):
+                came(chain, step)
+
+                @pl.when(step + 1 < steps)
+                def _():
+                    hop(chain, step + 1).start()
+
+                if each is not None:
+                    each(chain, step).start()
+
+    def ring_steps(chains, first, last, each=None):
         def body(step, carry):
-            for chain in chains:
-                steps = chain[3]
-
-                @pl.when(step < steps)
-                def _(chain=chain, steps=steps):
-                    came(chain, step)
-
-                    @pl.when(step + 1 < steps)
-                    def _():
-                        hop(chain, step + 1).start()
-
+            ring_step(chains, step, each)
             return carry
 
-        lax.fori_loop(0, far, body, 0)
+        if first < last:
+            lax.fori_loop(first, last, body, 0)
 
     def ring_drain(chains):
         for chain in chains:
@@ -270,20 +287,53 @@
 
             lax.fori_loop(0, chain[3], body, 0)
 
-    all_rows = pl.ds(0, units)
-    first_rows = pl.ds(0, units // 2)
-    last_rows = pl.ds(units // 2, units // 2)
+    upper = pl.ds(0, units // 2)
+    lower = pl.ds(units // 2, units // 2)
     weight_chains = [
-        (up_all, all_rows, True, far, 0),
-        (up_all, all_rows, False, near, 1),
-        (down_all, all_rows, True, near, 2),
-        (down_all, all_rows, False, far, 3),
+        (wide_all, upper, True, far, 0),
+        (wide_all, upper, False, near, 1),
+        (wide_all, lower, True, near, 2),
+        (wide_all, lower, False, far, 3),
+        (rest_all, upper, True, far, 4),
+        (rest_all, upper, False, near, 5),
+        (rest_all, lower, True, near, 6),
+        (rest_all, lower, False, far, 7),
     ]
-    head_chains = [
-        (head_all, first_rows, True, far, 4),
-        (head_all, first_rows, False, near, 5),
-        (head_all, last_rows, True, near, 6),
-        (head_all, last_rows, False, far, 7),
+    core = lax.rem(me_e, 2)
+    twin = me_e + 1 - 2 * core
+    quarter = units // 4
+
+    def head_rows(side, part):
+        return pl.ds(pl.multiple_of(side * 2 * quarter + part * quarter, 16), quarter)
+
+    def head_half(side):
+        return [
+            (head_all, head_rows(side, 0), True, far, 8),
+            (head_all, head_rows(side, 0), False, near, 9),
+            (head_all, head_rows(side, 1), True, near, 10),
+            (head_all, head_rows(side, 1), False, far, 11),
+        ]
+
+    head_chains = head_half(core)
+
+    def hand_over(chain, step):
+        buf, rows, to_right, steps, sem = chain
+        owner = lax.rem(me_d + (n_dp - 1 - step if to_right else step + 1), n_dp)
+        place = buf.at[owner, rows]
+        return remote(place, place, twin_send.at[sem - 8, step], twin_recv.at[sem - 8, step], "expert", twin)
+
+    def twins(chains, do):
+        for chain in chains:
+
+            def body(step, carry, chain=chain):
+                do(hand_over(chain, step))
+                return carry
+
+            lax.fori_loop(0, chain[3], body, 0)
+
+    pooled_chains = [
+        (pooled_all, pl.ds(0, cands), True, far, 20),
+        (pooled_all, pl.ds(0, cands), False, near, 21),
     ]
 
     def push(n, src, dst, p):
@@ -318,34 +368,47 @@
         mix_over_t[...] = jnp.transpose(table).astype(BF16)
 
     with jax.named_scope("weight_ring"):
-        ring_rest(weight_chains)
+        ring_steps(weight_chains, 0, far - 1)
+        ring_start(head_chains)
+        ring_steps(weight_chains, far - 1, far)
 
     with jax.named_scope("dispatch_wait"):
         expert_peers(lambda p: arrived(0, snd1, rcv1, p))
 
     with jax.named_scope("expert_forward"):
-        ring_start(head_chains)
-
-        def forward(g, carry):
+        ring_step(head_chains, 0, hand_over)
+        down_full[:, 0:rest] = rest_all[...].reshape(width, rest)
+        down_full[:, rest:lanes] = wide_all[:, :, rest:lanes].reshape(width, lanes - rest)
+
+        def no_column(rows):
+            lane = iota((rows, lanes), 1)
+            return (lane >= rest) & (lane < rest + spare)
+
+        def forward(g):
             main, over = unpack(rcv1, g)
-            rows = pl.ds(pl.multiple_of(g * g_rows, 16), g_rows)
+            rows = pl.ds(g * g_rows, g_rows)
             x = jnp.concatenate([main, over], axis=0)
             x_all[rows, :] = x
-            up_full = up_all[...].reshape(width, up.shape[2])
-            pre_act = dot(x, up_full)
+            natural = dot(x, wide_all[...].reshape(width, lanes))
+            pre_act = jnp.where(no_column(g_rows), 0.0, pltpu.roll(natural, lanes - spare, 1))
             pre[rows, :] = pre_act
             activated = (pre_act * jax.nn.sigmoid(pre_act)).astype(BF16)
             act[rows, :] = activated
-            out = dot(activated, down_all[...].reshape(width, down.shape[2]), 1, 1)
+            out = dot(activated, down_full[...], 1, 1)
             pack(snd2, g, out[0:g_main], out[g_main:g_rows])
             send_group(1, snd2, rcv2, g)
-            return carry
-
-        lax.fori_loop(0, groups, forward, 0)
+
+        head_at = 1
+        for g in range(groups):
+            forward(g)
+            if head_at < far:
+                ring_step(head_chains, head_at, hand_over)
+                head_at += 1
         keep_own(snd2, rcv2)
 
     with jax.named_scope("head_ring"):
-        ring_rest(head_chains)
+        ring_steps(head_chains, head_at, far, hand_over)
+        twins(head_half(1 - core), lambda copy: copy.wait_recv())
 
     with jax.named_scope("slope"):
 
@@ -353,7 +416,8 @@
             rows = pl.ds(pl.multiple_of(g * (g_rows // 4), 16), g_rows // 4)
             pre_act = pre[rows, :]
             sigmoid = jax.nn.sigmoid(pre_act)
-            pre[rows, :] = sigmoid * (1.0 + pre_act * (1.0 - sigmoid))
+            slope_of = sigmoid * (1.0 + pre_act * (1.0 - sigmoid))
+            pre[rows, :] = jnp.where(no_column(g_rows // 4), 0.0, slope_of)
             return carry
 
         lax.fori_loop(0, groups * 4, slope, 0)
@@ -392,6 +456,8 @@
         normed_high, normed_low = split(normed)
         pooled_sum = dot(member_t, normed_high) + dot(member_t, normed_low)
         pooled = (pooled_sum / counts).astype(BF16)
+        pooled_all[pl.ds(me_d, 1)] = pooled.reshape(1, cands, width)
+        ring_start(pooled_chains)
     with jax.named_scope("head_forward"):
         head_act = jnp.tanh(dot(pooled, head_all[...].reshape(hidden, width), 1, 1))
         scores = jnp.sum(head_act * ow_row, axis=1, keepdims=True)
@@ -403,6 +469,8 @@
         totals[pl.ds(me_d, 1)] = terms.reshape(1, 8, 128)
     with jax.named_scope("totals"):
         dp_peers(lambda p: push(1, totals.at[me_d], totals, p).start())
+        pooled_at = min(2, far)
+        ring_steps(pooled_chains, 0, pooled_at)
         dp_peers(lambda p: pushed(1, totals.at[me_d], totals, p))
     with jax.named_scope("head_backward"):
         total = jnp.sum(totals[...], axis=0)
@@ -435,16 +503,17 @@
         for k in range(hidden // 128):
             hid_snd[k] = hid_grad[:, k * 128 : (k + 1) * 128]
             out_snd[k] = jnp.broadcast_to(out_term[:, k * 128 : (k + 1) * 128], (8, 128))
-        pooled_all[pl.ds(me_d, 1)] = pooled.reshape(1, cands, width)
         hid_rcv[pl.ds(me_d, 1)] = hid_snd[pl.ds(me_d // 2, 1)]
         out_rcv[pl.ds(me_d, 1)] = out_snd[pl.ds(me_d // 2, 1)]
 
         def send_terms(p):
             push(2, hid_snd.at[p // 2], hid_rcv, p).start()
             push(3, out_snd.at[p // 2], out_rcv, p).start()
-            push(4, pooled_all.at[me_d], pooled_all, p).start()
 
         dp_peers(send_terms)
+
+    with jax.named_scope("pooled_ring"):
+        ring_steps(pooled_chains, pooled_at, far)
 
     with jax.named_scope("grad_wait"):
         expert_peers(lambda p: arrived(2, snd3, rcv3, p))
@@ -452,24 +521,32 @@
     tile = min(256, width)
     blocks = tile // units
 
-    def term(dst, a, b):
-        def body(f, carry):
-            part = dot(a[:, pl.ds(pl.multiple_of(f * tile, 128), tile)], b[...], 0, 0)
-            dst[pl.ds(f * blocks, blocks)] = part.astype(BF16).reshape(blocks, units, b.shape[1])
-            return carry
-
-        lax.fori_loop(0, width // tile, body, 0)
+    def down_part(f, carry):
+        part = dot(g_all[:, pl.ds(pl.multiple_of(f * tile, 128), tile)], act[...], 0, 0)
+        place = pl.ds(f * blocks, blocks)
+        down_sum[place] = part[:, 0:rest].astype(BF16).reshape(blocks, units, rest)
+        up_sum[place, :, rest:lanes] = part[:, rest:lanes].astype(BF16).reshape(blocks, units, lanes - rest)
+        return carry
+
+    def up_part(f, carry):
+        part = dot(x_all[:, pl.ds(pl.multiple_of(f * tile, 128), tile)], pre_grad[...], 0, 0)
+        place = pl.ds(f * blocks, blocks)
+        up_sum[place, :, 0:rest] = part[:, 0:rest].astype(BF16).reshape(blocks, units, rest)
+        below = up_sum[place, :, rest:lanes].astype(F32).reshape(tile, lanes - rest)
+        last = jnp.where(iota(below.shape, 1) < spare, pltpu.roll(below, spare, 1), part[:, rest:lanes])
+        up_sum[place, :, rest:lanes] = last.astype(BF16).reshape(blocks, units, lanes - rest)
+        return carry
 
     def sum_hop(chain, step):
-        own, to_right, steps, sem, slot = chain
+        own, ring, to_right, steps, sem, slot, rows = chain
         if isinstance(step, int) and step == 0:
             owner = lax.rem(me_d + (steps if to_right else n_dp - steps), n_dp)
-            src = own.at[owner]
+            src = own.at[owner, rows]
         else:
-            src = ring_buf.at[slot, step - 1]
+            src = ring.at[slot, step - 1, rows]
         return remote(
             src,
-            ring_buf.at[slot, step],
+            ring.at[slot, step, rows],
             ring_send.at[sem, step],
             ring_recv.at[sem, step],
             "dp",
@@ -477,14 +554,22 @@
         )
 
     def sum_came(chain, step):
-        own, to_right, steps, sem, slot = chain
-        place = ring_buf.at[slot, step]
+        own, ring, to_right, steps, sem, slot, rows = chain
+        place = ring.at[slot, step, rows]
         remote(
             place, place, ring_send.at[sem, step], ring_recv.at[sem, step], "dp", right if to_right else left
         ).wait_recv()
 
-    up_chains = [(up_sum, True, far, 8, 0), (up_sum, False, near, 9, 1)]
-    down_chains = [(down_sum, True, near, 10, 2), (down_sum, False, far, 11, 3)]
+    def sum_chains(own, ring, sem):
+        return [
+            (own, ring, True, far, sem, 0, upper),
+            (own, ring, False, near, sem + 1, 1, upper),
+            (own, ring, True, near, sem + 2, 0, lower),
+            (own, ring, False, far, sem + 3, 1, lower),
+        ]
+
+    up_chains = sum_chains(up_sum, up_ring, 12)
+    down_chains = sum_chains(down_sum, down_ring, 16)
 
     with jax.named_scope("down_term"):
 
@@ -495,7 +580,7 @@
             return carry
 
         lax.fori_loop(0, groups, gather, 0)
-        term(down_sum, g_all, act)
+        lax.fori_loop(0, width // tile, down_part, 0)
         for chain in down_chains:
             sum_hop(chain, 0).start()
 
@@ -503,12 +588,12 @@
 
         def backward(g, carry):
             rows = pl.ds(pl.multiple_of(g * g_rows, 16), g_rows)
-            act_grad = dot(g_all[rows, :], down_all[...].reshape(width, down.shape[2]))
+            act_grad = dot(g_all[rows, :], down_full[...])
             pre_grad[rows, :] = (act_grad * pre[rows, :]).astype(BF16)
             return carry
 
         lax.fori_loop(0, groups, backward, 0)
-        term(up_sum, x_all, pre_grad)
+        lax.fori_loop(0, width // tile, up_part, 0)
         for chain in up_chains:
             sum_hop(chain, 0).start()
 
@@ -518,7 +603,6 @@
         def got_terms(p):
             pushed(2, hid_snd.at[p // 2], hid_rcv, p)
             pushed(3, out_snd.at[p // 2], out_rcv, p)
-            pushed(4, pooled_all.at[me_d], pooled_all, p)
 
         dp_peers(got_terms)
         head_term[...] = dot(
@@ -552,17 +636,17 @@
     def sum_steps(first, last):
         def body(step, carry):
             for chain in down_chains + up_chains:
-                own, to_right, steps, sem, slot = chain
+                steps = chain[3]
 
                 @pl.when(step + 1 < steps)
                 def _(chain=chain):
-                    own, to_right, steps, sem, slot = chain
+                    own, ring, to_right, steps, sem, slot, rows = chain
                     sum_came(chain, step)
                     owner = lax.rem(
                         me_d + (steps - 1 - step if to_right else n_dp - (steps - 1) + step), n_dp
                     )
-                    total = ring_buf[slot, pl.ds(step, 1)].astype(F32) + own[pl.ds(owner, 1)].astype(F32)
-                    ring_buf[slot, pl.ds(step, 1)] = total.astype(BF16)
+                    total = ring[slot, pl.ds(step, 1), rows].astype(F32) + own[pl.ds(owner, 1), rows].astype(F32)
+                    ring[slot, pl.ds(step, 1), rows] = total.astype(BF16)
                     sum_hop(chain, step + 1).start()
 
             return carry
@@ -592,13 +676,21 @@
             grad_head[a * 16 : (a + 1) * 16, b * 128 : (b + 1) * 128] = whole_piece[q]
 
     with jax.named_scope("sum_end"):
-        for dst, chains in ((grad_down, down_chains), (grad_up, up_chains)):
-            total = chains[0][0][pl.ds(me_d, 1)].astype(F32)
-            for chain in chains:
-                own, to_right, steps, sem, slot = chain
-                sum_came(chain, steps - 1)
-                total = total + ring_buf[slot, steps - 1].astype(F32)[None]
-            dst[...] = total.astype(BF16)
+        sums = []
+        for chains in (down_chains, up_chains):
+            halves = []
+            for pair in (chains[0:2], chains[2:4]):
+                total = 0.0
+                for chain in pair:
+                    own, ring, to_right, steps, sem, slot, rows = chain
+                    sum_came(chain, steps - 1)
+                    total = total + ring[slot, steps - 1, rows].astype(F32)
+                halves.append(total + own[pl.ds(me_d, 1), rows][0].astype(F32))
+            sums.append(jnp.concatenate(halves, axis=0))
+        most, wide = sums
+        grad_up[...] = pltpu.roll(wide, spare, 1)[:, 0:ff].astype(BF16)[None]
+        whole = jnp.concatenate([most, pltpu.roll(wide[:, rest:lanes], spare, 1)], axis=1)
+        grad_down[...] = pltpu.roll(whole, spare, 1)[:, 0:ff].astype(BF16)[None]
 
     with jax.named_scope("drain"):
 
@@ -617,10 +709,10 @@
             push(1, totals.at[me_d], totals, p).wait_send()
             push(2, hid_snd.at[p // 2], hid_rcv, p).wait_send()
             push(3, out_snd.at[p // 2], out_rcv, p).wait_send()
-            push(4, pooled_all.at[me_d], pooled_all, p).wait_send()
 
         dp_peers(drain_dp)
-        ring_drain(weight_chains + head_chains)
+        ring_drain(weight_chains + head_chains + pooled_chains)
+        twins(head_chains, lambda copy: copy.wait_send())
         for chain in down_chains + up_chains:
             sum_hop(chain, 0).wait_send()
 
@@ -628,7 +720,12 @@
                 sum_hop(chain, step).wait_send()
                 return carry
 
-            lax.fori_loop(1, chain[2], body, 0)
+            lax.fori_loop(1, chain[3], body, 0)
+
+
+def hand_out(*refs):
+    for src, dst in zip(refs[:5], refs[5:]):
+        dst[...] = src[...]
 
 
 def local(
@@ -650,6 +747,8 @@
     n_exp = lax.axis_size("expert")
     toks, width = tokens.shape
     ff = up_weight.shape[2]
+    lanes = -(-ff // 128) * 128
+    rest = 2 * ff - lanes
     units = head_weight.shape[0]
     cands = list_ids.shape[1]
     slots = n_exp * (MAIN + OVER)
@@ -683,16 +782,18 @@
             pltpu.VMEM((2 * toks, n_exp * OVER), BF16),
             pltpu.VMEM((slots, width), BF16),
             pltpu.VMEM((slots, width), BF16),
-            pltpu.VMEM((slots, ff), F32),
-            pltpu.VMEM((slots, ff), BF16),
-            pltpu.VMEM((slots, ff), BF16),
-            pltpu.VMEM((n_dp, width // n_dp, ff), BF16),
-            pltpu.VMEM((n_dp, width // n_dp, ff), BF16),
+            pltpu.VMEM((slots, lanes), F32),
+            pltpu.VMEM((slots, lanes), BF16),
+            pltpu.VMEM((slots, lanes), BF16),
+            pltpu.VMEM((n_dp, width // n_dp, lanes), BF16),
+            pltpu.VMEM((n_dp, width // n_dp, rest), BF16),
+            pltpu.VMEM((width, lanes), BF16),
             pltpu.VMEM((n_dp, units, width), BF16),
             pltpu.VMEM((n_dp, 8, 128), F32),
-            pltpu.VMEM((n_dp, width // n_dp, ff), BF16),
-            pltpu.VMEM((n_dp, width // n_dp, ff), BF16),
-            pltpu.VMEM((4, steps, width // n_dp, ff), BF16),
+            pltpu.VMEM((n_dp, width // n_dp, lanes), BF16),
+            pltpu.VMEM((n_dp, width // n_dp, rest), BF16),
+            pltpu.VMEM((2, steps, width // n_dp, lanes), BF16),
+            pltpu.VMEM((2, steps, width // n_dp, rest), BF16),
             pltpu.VMEM((n_dp, 8, 128), F32),
             pltpu.VMEM((pairs, cands, 128), BF16),
             pltpu.VMEM((n_dp, cands, 128), BF16),
@@ -706,24 +807,26 @@
             pltpu.VMEM((n_exp, 8, 128), F32),
             pltpu.SemaphoreType.DMA((3, n_exp)),
             pltpu.SemaphoreType.DMA((3, n_exp)),
-            pltpu.SemaphoreType.DMA((12, steps)),
-            pltpu.SemaphoreType.DMA((12, steps)),
-            pltpu.SemaphoreType.DMA((5, n_dp)),
-            pltpu.SemaphoreType.DMA((5, n_dp)),
+            pltpu.SemaphoreType.DMA((22, steps)),
+            pltpu.SemaphoreType.DMA((22, steps)),
+            pltpu.SemaphoreType.DMA((4, n_dp)),
+            pltpu.SemaphoreType.DMA((4, n_dp)),
             pltpu.SemaphoreType.DMA((3, n_exp)),
             pltpu.SemaphoreType.DMA((3, n_exp)),
+            pltpu.SemaphoreType.DMA((4, steps)),
+            pltpu.SemaphoreType.DMA((4, steps)),
         ],
         compiler_params=pltpu.CompilerParams(
             collective_id=0, has_side_effects=True, vmem_limit_bytes=56 * 1024 * 1024
         ),
     )(
         tokens,
-        route_ids,
-        route_weights,
+        route_ids.T,
+        route_weights.T,
         up_weight,
         down_weight,
         head_weight,
-        jnp.concatenate([out_weight, out_weight]).reshape(1, 2 * units),
+        out_weight.reshape(1, units),
         pool_ids,
         list_ids,
         clicks,
@@ -731,7 +834,12 @@
         alpha_table.reshape(1, RANKS),
         beta_table.reshape(1, RANKS),
     )
-    grad_up, grad_down, grad_head, grad_out, list_loss = outs
+    grad_up, grad_down, grad_head, grad_out, list_loss = pl.pallas_call(
+        hand_out,
+        out_shape=[jax.ShapeDtypeStruct(o.shape, o.dtype) for o in outs],
+        in_specs=[vmem] * 5,
+        out_specs=[vmem] * 5,
+    )(*outs)
     return grad_up, grad_down, grad_head, grad_out.reshape(units), list_loss.reshape(1)
 
 

time: 181 us -> 168 us (0.928)
  local copies, waits for them, and re-layouts: 6.47 us -> 0 us
  Pallas kernels: 172 us -> 167 us
    pallas_call x1, Pallas kernels: 172 us -> 165 us  [local(): pl.pallas_call(functools.partial(kernel, n_dp, n_exp), out_shape=(jax.Sha...]
    unnamed x16 -> x0, local copies, waits for them, and re-layouts: 6.47 us -> none
    pallas_call x0 -> x1, Pallas kernels: none -> 2.45 us  [local(): pl.pallas_call(hand_out, out_shape=[jax.ShapeDtypeStruct(o.shape, o.dtype...]
where the time goes in v2:
time: 168 us
  Pallas kernels  167 us (99%)
    pallas_call x1, Pallas kernels, local(): pl.pallas_call(functools.partial(kernel, n_dp, n_exp), out_shape=(jax.Sha...  165 us

profile of v2, /device:TPU:28, one launch (start us, length us, event | category | flops | bytes accessed | tf_op | source)
XLA Modules:
  0.0 167.9 jit_solution(17691755025161724638)
XLA Ops:
  0.6 164.8 %shard_map.164 = (bf16[1,64,704]{2,1,0:T(8,128)(2,1)}, bf16[1,64,704]{2,1,0:T(8,128)(2,1)}, f32[64,1024]{1,0:T(8,128)}, f32[1,64]{1,0:T(1,128)}, f32[1,1]{1,0:T(1,128)}) custom-call(bf16[128,1024]{1,0:T(8,128)(2,1)} %tok.1, s32[4,128]{1,0:T(4,128)} %bitcast.7, f32[4,128]{1,0:T(4,128)} %bitcast.8, bf16[1,64,704]{2,1,0:T(8,128)(2,1)} %up.1, ...), custom_call_target="tpu_custom_call" | custom-call | tf_op jit(solution)/shard_map/pallas_call | solution.py:759
  165.5 2.4 %shard_map.165 = (bf16[1,64,704]{2,1,0:T(8,128)(2,1)}, bf16[1,64,704]{2,1,0:T(8,128)(2,1)}, f32[64,1024]{1,0:T(8,128)}, f32[1,64]{1,0:T(1,128)}, f32[1,1]{1,0:T(1,128)}) custom-call(bf16[1,64,704]{2,1,0:T(8,128)(2,1)} %get-tuple-element.15.refs_0_, bf16[1,64,704]{2,1,0:T(8,128)(2,1)} %get-tuple-element.16.refs_1_, f32[64,1024]{1,0:T(8,128)} %get-tuple-element.17.refs_2_, ...), custom_call_target="tpu_custom_call" | custom-call | tf_op jit(solution)/shard_map/pallas_call | solution.py:837

commit v3 on v2

--- a/solution.py
+++ b/solution.py
@@ -122,18 +122,20 @@
     right = lax.rem(me_d + 1, n_dp)
     left = lax.rem(me_d + n_dp - 1, n_dp)
 
-    def over_peers(axis, size, me, do):
+    def expert_peers(do):
         def body(k, carry):
-            do(lax.rem(me + k, size))
-            return carry
-
-        lax.fori_loop(1, size, body, 0)
-
-    def expert_peers(do):
-        over_peers("expert", n_exp, me_e, do)
+            do(lax.rem(me_e + k, n_exp))
+            return carry
+
+        lax.fori_loop(1, n_exp, body, 0)
 
     def dp_peers(do):
-        over_peers("dp", n_dp, me_d, do)
+        def body(k, carry):
+            away = n_dp // 2 + ((k + 1) // 2) * (1 - 2 * lax.rem(k, 2))
+            do(lax.rem(me_d + away, n_dp))
+            return carry
+
+        lax.fori_loop(0, n_dp - 1, body, 0)
 
     def remote(src, dst, send, recv, axis, peer):
         return pltpu.make_async_remote_copy(
@@ -146,10 +148,13 @@
         )
 
     def exchange(n, src, dst, p):
-        return remote(src.at[p], dst.at[me_e], a2a_send.at[n, p], a2a_recv.at[n, me_e], "expert", p)
-
-    def arrived(n, src, dst, p):
-        remote(src.at[p], dst.at[p], a2a_send.at[n, p], a2a_recv.at[n, p], "expert", p).wait_recv()
+        return remote(src.at[p], dst.at[me_e], a2a_send.at[n], a2a_recv.at[n], "expert", p)
+
+    next_e = lax.rem(me_e + 1, n_exp)
+
+    def exchanged(n, src, dst):
+        peers = pl.ds(0, n_exp - 1)
+        return remote(src.at[peers], dst.at[peers], a2a_send.at[n], a2a_recv.at[n], "expert", next_e)
 
     def send_group(n, src, dst, g):
         def body(k, carry):
@@ -240,7 +245,7 @@
         owner = lax.rem(me_d + (n_dp - step if to_right else step), n_dp)
         place = buf.at[owner, rows]
         return remote(
-            place, place, ring_send.at[sem, step], ring_recv.at[sem, step], "dp", right if to_right else left
+            place, place, ring_send.at[sem], ring_recv.at[sem, step], "dp", right if to_right else left
         )
 
     def came(chain, step):
@@ -248,7 +253,7 @@
         owner = lax.rem(me_d + (n_dp - 1 - step if to_right else step + 1), n_dp)
         place = buf.at[owner, rows]
         remote(
-            place, place, ring_send.at[sem, step], ring_recv.at[sem, step], "dp", right if to_right else left
+            place, place, ring_send.at[sem], ring_recv.at[sem, step], "dp", right if to_right else left
         ).wait_recv()
 
     def ring_start(chains):
@@ -279,13 +284,9 @@
             lax.fori_loop(first, last, body, 0)
 
     def ring_drain(chains):
-        for chain in chains:
-
-            def body(step, carry, chain=chain):
-                hop(chain, step).wait_send()
-                return carry
-
-            lax.fori_loop(0, chain[3], body, 0)
+        for buf, rows, to_right, steps, sem in chains:
+            place = buf.at[pl.ds(0, steps), rows]
+            remote(place, place, ring_send.at[sem], ring_recv.at[sem, 0], "dp", right).wait_send()
 
     upper = pl.ds(0, units // 2)
     lower = pl.ds(units // 2, units // 2)
@@ -320,16 +321,12 @@
         buf, rows, to_right, steps, sem = chain
         owner = lax.rem(me_d + (n_dp - 1 - step if to_right else step + 1), n_dp)
         place = buf.at[owner, rows]
-        return remote(place, place, twin_send.at[sem - 8, step], twin_recv.at[sem - 8, step], "expert", twin)
+        return remote(place, place, twin_send.at[sem - 8], twin_recv.at[sem - 8], "expert", twin)
 
     def twins(chains, do):
-        for chain in chains:
-
-            def body(step, carry, chain=chain):
-                do(hand_over(chain, step))
-                return carry
-
-            lax.fori_loop(0, chain[3], body, 0)
+        for buf, rows, to_right, steps, sem in chains:
+            place = buf.at[pl.ds(0, steps), rows]
+            do(remote(place, place, twin_send.at[sem - 8], twin_recv.at[sem - 8], "expert", twin))
 
     pooled_chains = [
         (pooled_all, pl.ds(0, cands), True, far, 20),
@@ -337,10 +334,11 @@
     ]
 
     def push(n, src, dst, p):
-        return remote(src, dst.at[me_d], dp_send.at[n, p], dp_recv.at[n, me_d], "dp", p)
-
-    def pushed(n, src, dst, p):
-        remote(src, dst.at[p], dp_send.at[n, p], dp_recv.at[n, p], "dp", p).wait_recv()
+        return remote(src, dst.at[me_d], dp_send.at[n], dp_recv.at[n], "dp", p)
+
+    def pushed(n, dst):
+        peers = pl.ds(0, n_dp - 1)
+        return remote(dst.at[peers], dst.at[peers], dp_send.at[n], dp_recv.at[n], "dp", right)
 
     with jax.named_scope("dispatch_send"):
         ring_start(weight_chains)
@@ -368,15 +366,25 @@
         mix_over_t[...] = jnp.transpose(table).astype(BF16)
 
     with jax.named_scope("weight_ring"):
-        ring_steps(weight_chains, 0, far - 1)
+        head_at = max(0, min(3, far - 1))
+        ring_steps(weight_chains, 0, far - 1 - head_at)
         ring_start(head_chains)
-        ring_steps(weight_chains, far - 1, far)
+        ring_steps(weight_chains, far - 1 - head_at, far - head_at)
+
+        def both_steps(k, carry):
+            ring_step(weight_chains, k + (far - head_at), None)
+            ring_step(head_chains, k, hand_over)
+            return carry
+
+        lax.fori_loop(0, head_at, both_steps, 0)
 
     with jax.named_scope("dispatch_wait"):
-        expert_peers(lambda p: arrived(0, snd1, rcv1, p))
+        exchanged(0, snd1, rcv1).wait_recv()
 
     with jax.named_scope("expert_forward"):
-        ring_step(head_chains, 0, hand_over)
+        if head_at < far:
+            ring_step(head_chains, head_at, hand_over)
+            head_at += 1
         down_full[:, 0:rest] = rest_all[...].reshape(width, rest)
         down_full[:, rest:lanes] = wide_all[:, :, rest:lanes].reshape(width, lanes - rest)
 
@@ -398,7 +406,6 @@
             pack(snd2, g, out[0:g_main], out[g_main:g_rows])
             send_group(1, snd2, rcv2, g)
 
-        head_at = 1
         for g in range(groups):
             forward(g)
             if head_at < far:
@@ -436,13 +443,13 @@
         alpha_of = jnp.sum(rank_hot * alpha[...], axis=1, keepdims=True)
         beta_of = jnp.sum(rank_hot * beta[...], axis=1, keepdims=True)
         corrected = (column(clicks[...].astype(F32), cands) - beta_of) / alpha_of
-        dp_peers(lambda p: pushed(0, ow_all.at[me_d], ow_all, p))
+        pushed(0, ow_all).wait_recv()
         ow_row = jnp.concatenate(
             [(ow_all[2 * k] + ow_all[2 * k + 1])[0:1] for k in range(hidden // 128)], axis=1
         )
 
     with jax.named_scope("return_wait"):
-        expert_peers(lambda p: arrived(1, snd2, rcv2, p))
+        exchanged(1, snd2, rcv2).wait_recv()
 
     with jax.named_scope("mix"):
         stacked = jnp.zeros((2 * toks, width), F32)
@@ -471,7 +478,7 @@
         dp_peers(lambda p: push(1, totals.at[me_d], totals, p).start())
         pooled_at = min(2, far)
         ring_steps(pooled_chains, 0, pooled_at)
-        dp_peers(lambda p: pushed(1, totals.at[me_d], totals, p))
+        pushed(1, totals).wait_recv()
     with jax.named_scope("head_backward"):
         total = jnp.sum(totals[...], axis=0)
         in_list = iota((1, 128), 1) < LISTS
@@ -516,7 +523,7 @@
         ring_steps(pooled_chains, pooled_at, far)
 
     with jax.named_scope("grad_wait"):
-        expert_peers(lambda p: arrived(2, snd3, rcv3, p))
+        exchanged(2, snd3, rcv3).wait_recv()
 
     tile = min(256, width)
     blocks = tile // units
@@ -547,7 +554,7 @@
         return remote(
             src,
             ring.at[slot, step, rows],
-            ring_send.at[sem, step],
+            ring_send.at[sem],
             ring_recv.at[sem, step],
             "dp",
             right if to_right else left,
@@ -557,7 +564,7 @@
         own, ring, to_right, steps, sem, slot, rows = chain
         place = ring.at[slot, step, rows]
         remote(
-            place, place, ring_send.at[sem, step], ring_recv.at[sem, step], "dp", right if to_right else left
+            place, place, ring_send.at[sem], ring_recv.at[sem, step], "dp", right if to_right else left
         ).wait_recv()
 
     def sum_chains(own, ring, sem):
@@ -600,11 +607,8 @@
     columns = width // 128
     with jax.named_scope("head_term"):
 
-        def got_terms(p):
-            pushed(2, hid_snd.at[p // 2], hid_rcv, p)
-            pushed(3, out_snd.at[p // 2], out_rcv, p)
-
-        dp_peers(got_terms)
+        pushed(2, hid_rcv).wait_recv()
+        pushed(3, out_rcv).wait_recv()
         head_term[...] = dot(
             hid_rcv[...].reshape(n_dp * cands, 128), pooled_all[...].reshape(n_dp * cands, width), 0, 0
         )
@@ -616,16 +620,17 @@
         out_piece[pl.ds(me_e, 1)] = jnp.sum(out_rcv[...], axis=0).reshape(1, 8, 128)
 
     def piece(p):
-        return remote(piece_snd.at[p], piece_rcv.at[me_e], exp_send.at[0, p], exp_recv.at[0, me_e], "expert", p)
+        return remote(piece_snd.at[p], piece_rcv.at[me_e], exp_send.at[0], exp_recv.at[0], "expert", p)
 
     def out_push(p):
-        return remote(out_piece.at[me_e], out_piece.at[me_e], exp_send.at[1, p], exp_recv.at[1, me_e], "expert", p)
+        return remote(out_piece.at[me_e], out_piece.at[me_e], exp_send.at[1], exp_recv.at[1], "expert", p)
 
     def whole_push(p):
-        return remote(whole_piece.at[me_e], whole_piece.at[me_e], exp_send.at[2, p], exp_recv.at[2, me_e], "expert", p)
-
-    def got(n, ref, p):
-        remote(ref.at[p], ref.at[p], exp_send.at[n, p], exp_recv.at[n, p], "expert", p).wait_recv()
+        return remote(whole_piece.at[me_e], whole_piece.at[me_e], exp_send.at[2], exp_recv.at[2], "expert", p)
+
+    def got(n, ref):
+        peers = pl.ds(0, n_exp - 1)
+        return remote(ref.at[peers], ref.at[peers], exp_send.at[n], exp_recv.at[n], "expert", next_e)
 
     def send_pieces(p):
         piece(p).start()
@@ -658,7 +663,7 @@
         sum_steps(0, middle)
 
     with jax.named_scope("head_pieces"):
-        expert_peers(lambda p: got(0, piece_rcv, p))
+        got(0, piece_rcv).wait_recv()
         whole_piece[pl.ds(me_e, 1)] = jnp.sum(piece_rcv[...].astype(F32), axis=0).reshape(1, 16, 128)
         expert_peers(lambda p: whole_push(p).start())
 
@@ -666,11 +671,11 @@
         sum_steps(middle, far - 1)
 
     with jax.named_scope("head_out"):
-        expert_peers(lambda p: got(1, out_piece, p))
+        got(1, out_piece).wait_recv()
         out_all = jnp.sum(out_piece[...], axis=0)[0:1]
         out_pair = jnp.where(parity == 0, out_all, pltpu.roll(out_all, 128 - units, 1))
         grad_out[...] = out_pair[:, 0:units]
-        expert_peers(lambda p: got(2, whole_piece, p))
+        got(2, whole_piece).wait_recv()
         for q in range(n_exp):
             a, b = q // columns, q % columns
             grad_head[a * 16 : (a + 1) * 16, b * 128 : (b + 1) * 128] = whole_piece[q]
@@ -693,34 +698,18 @@
         grad_down[...] = pltpu.roll(whole, spare, 1)[:, 0:ff].astype(BF16)[None]
 
     with jax.named_scope("drain"):
-
-        def drain_expert(p):
-            exchange(0, snd1, rcv1, p).wait_send()
-            exchange(1, snd2, rcv2, p).wait_send()
-            exchange(2, snd3, rcv3, p).wait_send()
-            piece(p).wait_send()
-            out_push(p).wait_send()
-            whole_push(p).wait_send()
-
-        expert_peers(drain_expert)
-
-        def drain_dp(p):
-            push(0, ow_all.at[me_d], ow_all, p).wait_send()
-            push(1, totals.at[me_d], totals, p).wait_send()
-            push(2, hid_snd.at[p // 2], hid_rcv, p).wait_send()
-            push(3, out_snd.at[p // 2], out_rcv, p).wait_send()
-
-        dp_peers(drain_dp)
+        exchanged(0, snd1, rcv1).wait_send()
+        exchanged(1, snd2, rcv2).wait_send()
+        exchanged(2, snd3, rcv3).wait_send()
+        for n, ref in enumerate((ow_all, totals, hid_rcv, out_rcv)):
+            pushed(n, ref).wait_send()
+        for n, ref in enumerate((piece_rcv, out_piece, whole_piece)):
+            got(n, ref).wait_send()
         ring_drain(weight_chains + head_chains + pooled_chains)
         twins(head_chains, lambda copy: copy.wait_send())
-        for chain in down_chains + up_chains:
-            sum_hop(chain, 0).wait_send()
-
-            def body(step, carry, chain=chain):
-                sum_hop(chain, step).wait_send()
-                return carry
-
-            lax.fori_loop(1, chain[3], body, 0)
+        for own, ring, to_right, steps, sem, slot, rows in down_chains + up_chains:
+            place = ring.at[slot, pl.ds(0, steps), rows]
+            remote(place, place, ring_send.at[sem], ring_recv.at[sem, 0], "dp", right).wait_send()
 
 
 def hand_out(*refs):
@@ -805,16 +794,16 @@
             pltpu.VMEM((n_exp, 16, 128), BF16),
             pltpu.VMEM((n_exp, 16, 128), F32),
             pltpu.VMEM((n_exp, 8, 128), F32),
-            pltpu.SemaphoreType.DMA((3, n_exp)),
-            pltpu.SemaphoreType.DMA((3, n_exp)),
+            pltpu.SemaphoreType.DMA((3,)),
+            pltpu.SemaphoreType.DMA((3,)),
+            pltpu.SemaphoreType.DMA((22,)),
             pltpu.SemaphoreType.DMA((22, steps)),
-            pltpu.SemaphoreType.DMA((22, steps)),
-            pltpu.SemaphoreType.DMA((4, n_dp)),
-            pltpu.SemaphoreType.DMA((4, n_dp)),
-            pltpu.SemaphoreType.DMA((3, n_exp)),
-            pltpu.SemaphoreType.DMA((3, n_exp)),
-            pltpu.SemaphoreType.DMA((4, steps)),
-            pltpu.SemaphoreType.DMA((4, steps)),
+            pltpu.SemaphoreType.DMA((4,)),
+            pltpu.SemaphoreType.DMA((4,)),
+            pltpu.SemaphoreType.DMA((3,)),
+            pltpu.SemaphoreType.DMA((3,)),
+            pltpu.SemaphoreType.DMA((4,)),
+            pltpu.SemaphoreType.DMA((4,)),
         ],
         compiler_params=pltpu.CompilerParams(
             collective_id=0, has_side_effects=True, vmem_limit_bytes=56 * 1024 * 1024

time: 168 us -> 157 us (0.935)
  Pallas kernels: 167 us -> 157 us
    pallas_call x1, Pallas kernels: 165 us -> 154 us  [local(): pl.pallas_call(functools.partial(kernel, n_dp, n_exp), out_shape=(jax.Sha...]
where the time goes in v3:
time: 157 us
  Pallas kernels  157 us (100%)
    pallas_call x1, Pallas kernels, local(): pl.pallas_call(functools.partial(kernel, n_dp, n_exp), out_shape=(jax.Sha...  154 us

profile of v3, /device:TPU:28, one launch (start us, length us, event | category | flops | bytes accessed | tf_op | source)
XLA Modules:
  0.0 157.3 jit_solution(9771009806632699355)
XLA Ops:
  0.6 154.2 %shard_map.164 = (bf16[1,64,704]{2,1,0:T(8,128)(2,1)}, bf16[1,64,704]{2,1,0:T(8,128)(2,1)}, f32[64,1024]{1,0:T(8,128)}, f32[1,64]{1,0:T(1,128)}, f32[1,1]{1,0:T(1,128)}) custom-call(bf16[128,1024]{1,0:T(8,128)(2,1)} %tok.1, s32[4,128]{1,0:T(4,128)} %bitcast.7, f32[4,128]{1,0:T(4,128)} %bitcast.8, bf16[1,64,704]{2,1,0:T(8,128)(2,1)} %up.1, ...), custom_call_target="tpu_custom_call" | custom-call | tf_op jit(solution)/shard_map/pallas_call | solution.py:748
  154.8 2.4 %shard_map.165 = (bf16[1,64,704]{2,1,0:T(8,128)(2,1)}, bf16[1,64,704]{2,1,0:T(8,128)(2,1)}, f32[64,1024]{1,0:T(8,128)}, f32[1,64]{1,0:T(1,128)}, f32[1,1]{1,0:T(1,128)}) custom-call(bf16[1,64,704]{2,1,0:T(8,128)(2,1)} %get-tuple-element.15.refs_0_, bf16[1,64,704]{2,1,0:T(8,128)(2,1)} %get-tuple-element.16.refs_1_, f32[64,1024]{1,0:T(8,128)} %get-tuple-element.17.refs_2_, ...), custom_call_target="tpu_custom_call" | custom-call | tf_op jit(solution)/shard_map/pallas_call | solution.py:826

commit v4 on v3

--- a/solution.py
+++ b/solution.py
@@ -525,7 +525,7 @@
     with jax.named_scope("grad_wait"):
         exchanged(2, snd3, rcv3).wait_recv()
 
-    tile = min(256, width)
+    tile = min(1024, width)
     blocks = tile // units
 
     def down_part(f, carry):

time: 157 us -> 156 us (level)
  the two profiles are of different devices: /device:TPU:28 before, /device:TPU:4 now
where the time goes in v4:
time: 156 us
  Pallas kernels  155 us (99%)
    pallas_call x1, Pallas kernels, local(): pl.pallas_call(functools.partial(kernel, n_dp, n_exp), out_shape=(jax.Sha...  152 us

profile of v4, /device:TPU:4, one launch (start us, length us, event | category | flops | bytes accessed | tf_op | source)
XLA Modules:
  0.0 155.5 jit_solution(12405562347764888621)
XLA Ops:
  0.6 152.4 %shard_map.164 = (bf16[1,64,704]{2,1,0:T(8,128)(2,1)}, bf16[1,64,704]{2,1,0:T(8,128)(2,1)}, f32[64,1024]{1,0:T(8,128)}, f32[1,64]{1,0:T(1,128)}, f32[1,1]{1,0:T(1,128)}) custom-call(bf16[128,1024]{1,0:T(8,128)(2,1)} %tok.1, s32[4,128]{1,0:T(4,128)} %bitcast.7, f32[4,128]{1,0:T(4,128)} %bitcast.8, bf16[1,64,704]{2,1,0:T(8,128)(2,1)} %up.1, ...), custom_call_target="tpu_custom_call" | custom-call | tf_op jit(solution)/shard_map/pallas_call | solution.py:748
  153.1 2.4 %shard_map.165 = (bf16[1,64,704]{2,1,0:T(8,128)(2,1)}, bf16[1,64,704]{2,1,0:T(8,128)(2,1)}, f32[64,1024]{1,0:T(8,128)}, f32[1,64]{1,0:T(1,128)}, f32[1,1]{1,0:T(1,128)}) custom-call(bf16[1,64,704]{2,1,0:T(8,128)(2,1)} %get-tuple-element.15.refs_0_, bf16[1,64,704]{2,1,0:T(8,128)(2,1)} %get-tuple-element.16.refs_1_, f32[64,1024]{1,0:T(8,128)} %get-tuple-element.17.refs_2_, ...), custom_call_target="tpu_custom_call" | custom-call | tf_op jit(solution)/shard_map/pallas_call | solution.py:826

commit v5 on v4

--- a/solution.py
+++ b/solution.py
@@ -593,13 +593,7 @@
 
     with jax.named_scope("up_term"):
 
-        def backward(g, carry):
-            rows = pl.ds(pl.multiple_of(g * g_rows, 16), g_rows)
-            act_grad = dot(g_all[rows, :], down_full[...])
-            pre_grad[rows, :] = (act_grad * pre[rows, :]).astype(BF16)
-            return carry
-
-        lax.fori_loop(0, groups, backward, 0)
+        pre_grad[...] = (dot(g_all[...], down_full[...]) * pre[...]).astype(BF16)
         lax.fori_loop(0, width // tile, up_part, 0)
         for chain in up_chains:
             sum_hop(chain, 0).start()

time: 156 us -> 156 us (level)
  the two profiles are of different devices: /device:TPU:4 before, /device:TPU:28 now
where the time goes in v5:
time: 156 us; the launch traced here: 155 us
  Pallas kernels  155 us (99%)
    pallas_call x1, Pallas kernels, local(): pl.pallas_call(functools.partial(kernel, n_dp, n_exp), out_shape=(jax.Sha...  152 us

profile of v5, /device:TPU:28, one launch (start us, length us, event | category | flops | bytes accessed | tf_op | source)
XLA Modules:
  0.0 155.5 jit_solution(15864850521575532640)
XLA Ops:
  0.6 152.4 %shard_map.164 = (bf16[1,64,704]{2,1,0:T(8,128)(2,1)}, bf16[1,64,704]{2,1,0:T(8,128)(2,1)}, f32[64,1024]{1,0:T(8,128)}, f32[1,64]{1,0:T(1,128)}, f32[1,1]{1,0:T(1,128)}) custom-call(bf16[128,1024]{1,0:T(8,128)(2,1)} %tok.1, s32[4,128]{1,0:T(4,128)} %bitcast.7, f32[4,128]{1,0:T(4,128)} %bitcast.8, bf16[1,64,704]{2,1,0:T(8,128)(2,1)} %up.1, ...), custom_call_target="tpu_custom_call" | custom-call | tf_op jit(solution)/shard_map/pallas_call | solution.py:742
  153.0 2.4 %shard_map.165 = (bf16[1,64,704]{2,1,0:T(8,128)(2,1)}, bf16[1,64,704]{2,1,0:T(8,128)(2,1)}, f32[64,1024]{1,0:T(8,128)}, f32[1,64]{1,0:T(1,128)}, f32[1,1]{1,0:T(1,128)}) custom-call(bf16[1,64,704]{2,1,0:T(8,128)(2,1)} %get-tuple-element.15.refs_0_, bf16[1,64,704]{2,1,0:T(8,128)(2,1)} %get-tuple-element.16.refs_1_, f32[64,1024]{1,0:T(8,128)} %get-tuple-element.17.refs_2_, ...), custom_call_target="tpu_custom_call" | custom-call | tf_op jit(solution)/shard_map/pallas_call | solution.py:820
